TPU v7x, 512 devices: a whole 4x4x16 slice. The times are simulated.
512 devices in a mesh: bx: 8 (over x, core), by: 16 (over z), rhs: 4 (over y).
Axes of the slice: x: 4, y: 4, z: 16, core: 2. Of those that a mesh axis runs over, the one named last changes fastest.
Arguments:
- rhs_nodes: float32 [8, 16, 64, 256], P('bx', 'by', 'rhs'), may hold values from -6 to 6
- forward: float32 [8, 16, 64, 256], P('bx', 'by', 'rhs'), may hold values from -6 to 6
- leaf_map: float32 [8, 16, 256, 256], P('bx', 'by'), may hold values from -0.375 to 0.375
- derivative: float32 [8, 16, 256, 256], P('bx', 'by'), may hold values from -0.375 to 0.375
- node_panel: int32 [8, 16, 256], P('bx', 'by'), may hold values from 0 to 15, never falling along the last dimension, each value on 1 to 32 neighbouring positions
- order_one: int32 [8, 16, 256], P('bx', 'by'), may hold values from 0 to 255, each once within a row
- near_one: int32 [8, 16, 9], P('bx', 'by'), may hold values 0 or 1
- interp_one: float32 [8, 16, 128, 128], P('bx', 'by'), may hold values from -0.25 to 0.25
- solve_one: float32 [8, 16, 128, 128], P('bx', 'by')
- couple_one: float32 [8, 16, 9, 128, 128], P('bx', 'by'), may hold values from -0.09375 to 0.09375
- back_one: float32 [8, 16, 128, 128], P('bx', 'by'), may hold values from -0.25 to 0.25
- spread_one: float32 [8, 16, 9, 128, 128], P('bx', 'by'), may hold values from -0.09375 to 0.09375
- order_two: int32 [8, 16, 256], P('bx', 'by'), may hold values from 0 to 255, as said below
- interp_two: float32 [8, 16, 128, 64], P('bx', 'by'), may hold values from -0.25 to 0.25
- solve_two: float32 [8, 16, 128, 64], P('bx', 'by')
- couple_two: float32 [8, 16, 9, 128, 64], P('bx', 'by'), may hold values from -0.09375 to 0.09375
- back_two: float32 [8, 16, 128, 64], P('bx', 'by'), may hold values from -0.25 to 0.25
- spread_two: float32 [8, 16, 9, 128, 64], P('bx', 'by'), may hold values from -0.09375 to 0.09375
- order_three: int32 [8, 16, 256], P('bx', 'by'), may hold values from 0 to 255, as said below
- interp_three: float32 [8, 16, 128, 32], P('bx', 'by'), may hold values from -0.25 to 0.25
- solve_three: float32 [8, 16, 128, 32], P('bx', 'by')
- couple_three: float32 [8, 16, 9, 128, 32], P('bx', 'by'), may hold values from -0.09375 to 0.09375
- back_three: float32 [8, 16, 128, 32], P('bx', 'by'), may hold values from -0.25 to 0.25
- spread_three: float32 [8, 16, 9, 128, 32], P('bx', 'by'), may hold values from -0.09375 to 0.09375
- top_three: float32 [8, 16, 128, 32], P('bx', 'by')
Outputs:
- adjoint: float32 [8, 16, 64, 256], P('bx', 'by', 'rhs')
- gradient: float32 [8, 16, 16], P('bx', 'by', 'rhs')
Inputs may be any that keep to these rules, and one draw needn't show every extreme that they name: `order_one`: each box's row is a permutation; the first 128 entries are its skeleton set, the rest its redundant set. `order_two`: each row is a permutation of the candidates of a second-level box; rows 2m and 2m + 1 of the same x are equal. `order_three`: each row is a permutation of the candidates of a third-level box; the four rows of one third-level box are equal. `node_panel`: never falling along a box's nodes; every panel has one or more nodes.
All inputs are finite; a program needn't handle non-finite values. No bound on the sum of `near_one` on one device may be relied on, other than what follows from the above.
Results may differ from a plain program's by a relative error of at most 0.00022.
Values sent between devices are 32-bit elements; how exact they have to be, the bound alone decides.
No kernel may reach another device: no remote copies, remote signals or barrier semaphores. Data moves between devices by JAX's collectives and lax.ppermute only.
A program may use at most 64 MiB of HBM per device.

v0:
```python
import jax
import jax.numpy as jnp
from jax import lax
from jax.sharding import PartitionSpec as P

PANELS = 16


highest = lax.Precision.HIGHEST


def from_behind(shard, axis, by):
    size = lax.axis_size(axis)
    pairs = [(i, i + by) for i in range(size) if 0 <= i + by < size]
    return lax.ppermute(shard, axis, pairs)


def swapped(shard, axis, apart):
    return lax.ppermute(shard, axis, [(i, i ^ 1 << apart) for i in range(lax.axis_size(axis))])


def matmul(left, right):
    return jnp.matmul(left, right, precision=highest)


def contract(stacked, blocks):
    return jnp.einsum("ncr,nrk->ck", stacked, blocks, precision=highest)


def picked_cols(values, order):
    return jnp.take(values, order, axis=1)


def placed_cols(values, order):
    return jnp.take(values, jnp.argsort(order), axis=1)


def row_move(values, amount):
    return from_behind(values, "by", amount)


def col_move(values, amount):
    return from_behind(values, "bx", amount)


def beside_all(values, rows_step, cols_step):
    column = jnp.stack([row_move(values, rows_step), values, row_move(values, -rows_step)])
    block = jnp.stack([col_move(column, cols_step), column, col_move(column, -cols_step)])
    return block.reshape((9,) + values.shape)


def nearby_one(values):
    stacked = beside_all(values, 1, 1)
    return stacked


def in_order(values, other, first):
    return jnp.where(
        first, jnp.concatenate([values, other], -1), jnp.concatenate([other, values], -1)
    )


def join_rows(values):
    other = swapped(values, "by", 0)
    return in_order(values, other, lax.axis_index("by") % 2 == 0)


def join_cols(values):
    other = swapped(values, "bx", 0)
    return in_order(values, other, lax.axis_index("bx") % 2 == 0)


def on_device(
    rhs_nodes,
    forward,
    leaf_map,
    derivative,
    node_panel,
    order_one,
    near_one,
    interp_one,
    solve_one,
    couple_one,
    back_one,
    spread_one,
    order_two,
    interp_two,
    solve_two,
    couple_two,
    back_two,
    spread_two,
    order_three,
    interp_three,
    solve_three,
    couple_three,
    back_three,
    spread_three,
    top_three,
):
    skeletons = interp_one.shape[-1]
    row_half = lax.axis_index("by") % 2
    col_half = lax.axis_index("bx") % 2
    weights = near_one[0, 0].astype(jnp.float32)[:, None, None]
    field = matmul(forward[0, 0], derivative[0, 0])
    cand = jnp.matmul(rhs_nodes[0, 0], leaf_map[0, 0].T, precision=highest)
    picked = picked_cols(cand, order_one[0, 0])
    redund = picked[:, skeletons:]
    zone_one = matmul(redund, solve_one[0, 0])
    skel_one = (
        picked[:, :skeletons]
        - matmul(redund, interp_one[0, 0])
        - contract(weights * nearby_one(zone_one), couple_one[0, 0])
    )
    half = skeletons // 2
    picked = picked_cols(join_rows(skel_one), order_two[0, 0])
    redund_two = picked[:, skeletons:]
    zone_half = matmul(redund_two, solve_two[0, 0])
    zone_two = join_rows(zone_half)
    own_half = lax.dynamic_slice_in_dim(picked, row_half * half, half, 1)
    skel_half = (
        own_half
        - matmul(redund_two, interp_two[0, 0])
        - contract(beside_all(zone_two, 2, 1), couple_two[0, 0])
    )
    picked = picked_cols(join_cols(join_rows(skel_half)), order_three[0, 0])
    redund_three = picked[:, skeletons:]
    quarter = skeletons // 4
    zone_part = matmul(redund_three, solve_three[0, 0])
    zone_three = join_cols(join_rows(zone_part))
    own_part = lax.dynamic_slice_in_dim(picked, (2 * col_half + row_half) * quarter, quarter, 1)
    skel_part = (
        own_part
        - matmul(redund_three, interp_three[0, 0])
        - contract(beside_all(zone_three, 2, 2), couple_three[0, 0])
    )
    skel_three = join_cols(join_rows(skel_part))
    value_three = join_cols(join_rows(matmul(skel_three, top_three[0, 0])))
    rest_part = (
        zone_part
        - matmul(value_three, back_three[0, 0])
        - contract(beside_all(value_three, 2, 2), spread_three[0, 0])
    )
    rest_three = join_cols(join_rows(rest_part))
    final_three = placed_cols(jnp.concatenate([value_three, rest_three], -1), order_three[0, 0])
    value_two = lax.dynamic_slice_in_dim(final_three, col_half * skeletons, skeletons, 1)
    rest_half = (
        zone_half
        - matmul(value_two, back_two[0, 0])
        - contract(beside_all(value_two, 2, 1), spread_two[0, 0])
    )
    final_two = placed_cols(jnp.concatenate([value_two, join_rows(rest_half)], -1), order_two[0, 0])
    value_one = lax.dynamic_slice_in_dim(final_two, row_half * skeletons, skeletons, 1)
    rest_one = (
        zone_one
        - matmul(value_one, back_one[0, 0])
        - contract(weights * nearby_one(value_one), spread_one[0, 0])
    )
    final_one = placed_cols(jnp.concatenate([value_one, rest_one], -1), order_one[0, 0])
    adjoint = matmul(final_one, leaf_map[0, 0])
    total_cols = lax.axis_size("rhs") * rhs_nodes.shape[2]
    summed = jnp.sum(adjoint * field, axis=0) / total_cols
    member = (node_panel[0, 0][:, None] == jnp.arange(PANELS, dtype=jnp.int32)[None, :]).astype(
        jnp.float32
    )
    partial_sum = jnp.matmul(summed, member, precision=highest)
    shares = lax.psum_scatter(partial_sum[None, None], "rhs", scatter_dimension=2, tiled=True)
    return (adjoint[None, None], shares)


def solution(mesh):
    placed = (
        P("bx", "by", "rhs", None),
        P("bx", "by", "rhs", None),
        P("bx", "by", None, None),
        P("bx", "by", None, None),
        P("bx", "by", None),
        P("bx", "by", None),
        P("bx", "by", None),
        P("bx", "by", None, None),
        P("bx", "by", None, None),
        P("bx", "by", None, None, None),
        P("bx", "by", None, None),
        P("bx", "by", None, None, None),
        P("bx", "by", None),
        P("bx", "by", None, None),
        P("bx", "by", None, None),
        P("bx", "by", None, None, None),
        P("bx", "by", None, None),
        P("bx", "by", None, None, None),
        P("bx", "by", None),
        P("bx", "by", None, None),
        P("bx", "by", None, None),
        P("bx", "by", None, None, None),
        P("bx", "by", None, None),
        P("bx", "by", None, None, None),
        P("bx", "by", None, None),
    )
    return jax.shard_map(
        on_device,
        mesh=mesh,
        in_specs=placed,
        out_specs=(P("bx", "by", "rhs", None), P("bx", "by", "rhs")),
        check_vma=False,
    )
```

profile of v0, /device:TPU:1, one launch (start us, length us, event | category | flops | bytes accessed | tf_op | source)
XLA Modules:
  0.0 209.9 jit_solution(5558814842206284055)
XLA Ops:
  0.7 3.9 %sort.47 = (s32[256]{0:T(256)}, s32[256]{0:T(256)S(1)}) sort(s32[256]{0:T(256)} %bitcast.203, s32[256]{0:T(256)S(1)} %iota.16), dimensions={0}, to_apply=%region_2.4 | sort | flops 2048 | bytes 4096 | tf_op jit(solution)/shard_map/jit(argsort)/sort | solution.py:35
  5.3 1.3 fusion.14
  8.3 1.3 collective-permute-start.1
  9.6 5.0 %collective-permute-start = (f32[16,128]{1,0:T(8,128)S(1)}, f32[16,128]{1,0:T(8,128)S(1)}, u32[]{:S(2)}, u32[]{:S(2)}) collective-permute-start(f32[16,128]{1,0:T(8,128)S(1)} %fusion.21), channel_id=1, source_target_pairs={{0,4},{4,8},{8,12},{12,16},{16,20},{20,24},{24,28},{28,32},{32,36}... | collective-permute-start | bytes 24584 | tf_op jit(solution)/shard_map/ppermute | solution.py:15
  15.4 4.7 %collective-permute-start.2 = (f32[3,16,128]{2,1,0:T(8,128)S(1)}, f32[3,16,128]{2,1,0:T(8,128)S(1)}, u32[]{:S(2)}, u32[]{:S(2)}) collective-permute-start(f32[3,16,128]{2,1,0:T(8,128)S(1)} %get-tuple-element.20), channel_id=1, source_target_pairs={{0,64},{64,128},{128,192},{192,256},{256,320},{320,384},{384,448},... | collective-permute-start | bytes 73736 | tf_op jit(solution)/shard_map/ppermute | solution.py:15
  20.2 5.6 %collective-permute-start.3 = (f32[3,16,128]{2,1,0:T(8,128)S(1)}, f32[3,16,128]{2,1,0:T(8,128)S(1)}, u32[]{:S(2)}, u32[]{:S(2)}) collective-permute-start(f32[3,16,128]{2,1,0:T(8,128)S(1)} %get-tuple-element.20), channel_id=1, source_target_pairs={{64,0},{128,64},{192,128},{256,192},{320,256},{384,320},{448,384},... | collective-permute-start | bytes 73736 | tf_op jit(solution)/shard_map/ppermute | solution.py:15
  27.1 3.9 %collective-permute-start.4 = (f32[16,128]{1,0:T(8,128)S(1)}, f32[16,128]{1,0:T(8,128)S(1)}, u32[]{:S(2)}, u32[]{:S(2)}) collective-permute-start(f32[16,128]{1,0:T(8,128)S(1)} %fusion.6), channel_id=1, source_target_pairs={{0,4},{4,0},{8,12},{12,8},{16,20},{20,16},{24,28},{28,24},{32,36},... | collective-permute-start | bytes 24584 | tf_op jit(solution)/shard_map/ppermute | solution.py:19
  31.0 1.0 collective-permute-done.4
  33.1 3.4 %collective-permute-start.5 = (f32[16,64]{1,0:T(8,128)S(1)}, f32[16,64]{1,0:T(8,128)S(1)}, u32[]{:S(2)}, u32[]{:S(2)}) collective-permute-start(f32[16,64]{1,0:T(8,128)S(1)} %fusion.28), channel_id=1, source_target_pairs={{0,4},{4,0},{8,12},{12,8},{16,20},{20,16},{24,28},{28,24},{32,36},... | collective-permute-start | bytes 12296 | tf_op jit(solution)/shard_map/ppermute | solution.py:19
  36.5 3.2 %sort.45 = (s32[256]{0:T(256)}, s32[256]{0:T(256)S(1)}) sort(s32[256]{0:T(256)S(1)} %bitcast.197, s32[256]{0:T(256)S(1)} %iota.14), dimensions={0}, to_apply=%region_0.2 | sort | flops 2048 | bytes 4096 | tf_op jit(solution)/shard_map/jit(argsort)/sort | solution.py:35
  39.8 4.5 %collective-permute-start.6 = (f32[16,128]{1,0:T(8,128)S(1)}, f32[16,128]{1,0:T(8,128)S(1)}, u32[]{:S(2)}, u32[]{:S(2)}) collective-permute-start(f32[16,128]{1,0:T(8,128)S(1)} %maximum_select_fusion.2), channel_id=1, source_target_pairs={{0,8},{4,12},{8,16},{12,20},{16,24},{20,28},{24,32},{28,36},{32,40... | collective-permute-start | bytes 24584 | tf_op jit(solution)/shard_map/ppermute | solution.py:15
  44.3 1.3 collective-permute-start.7
  45.6 5.1 %collective-permute-done.7 = f32[16,128]{1,0:T(8,128)S(1)} collective-permute-done((f32[16,128]{1,0:T(8,128)S(1)}, f32[16,128]{1,0:T(8,128)S(1)}, u32[]{:S(2)}, u32[]{:S(2)}) %collective-permute-start.7) | collective-permute-done | bytes 8224 | tf_op jit(solution)/shard_map/ppermute | solution.py:15
  50.7 4.4 %collective-permute-start.8 = (f32[3,16,128]{2,1,0:T(8,128)S(1)}, f32[3,16,128]{2,1,0:T(8,128)S(1)}, u32[]{:S(2)}, u32[]{:S(2)}) collective-permute-start(f32[3,16,128]{2,1,0:T(8,128)S(1)} %get-tuple-element.18), channel_id=1, source_target_pairs={{0,64},{64,128},{128,192},{192,256},{256,320},{320,384},{384,448},... | collective-permute-start | bytes 73736 | tf_op jit(solution)/shard_map/ppermute | solution.py:15
  55.1 1.9 collective-permute-start.9
  57.1 3.2 %collective-permute-done.9 = f32[3,16,128]{2,1,0:T(8,128)S(1)} collective-permute-done((f32[3,16,128]{2,1,0:T(8,128)S(1)}, f32[3,16,128]{2,1,0:T(8,128)S(1)}, u32[]{:S(2)}, u32[]{:S(2)}) %collective-permute-start.9) | collective-permute-done | bytes 24608 | tf_op jit(solution)/shard_map/ppermute | solution.py:15
  61.1 3.0 %collective-permute-start.10 = (f32[16,64]{1,0:T(8,128)S(1)}, f32[16,64]{1,0:T(8,128)S(1)}, u32[]{:S(2)}, u32[]{:S(2)}) collective-permute-start(f32[16,64]{1,0:T(8,128)S(1)} %fusion.5), channel_id=1, source_target_pairs={{0,4},{4,0},{8,12},{12,8},{16,20},{20,16},{24,28},{28,24},{32,36},... | collective-permute-start | bytes 12296 | tf_op jit(solution)/shard_map/ppermute | solution.py:19
  64.1 1.5 collective-permute-done.10
  65.7 1.9 collective-permute-start.11
  67.6 1.1 collective-permute-done.11
  70.5 2.9 %collective-permute-start.12 = (f32[16,32]{1,0:T(8,128)S(1)}, f32[16,32]{1,0:T(8,128)S(1)}, u32[]{:S(2)}, u32[]{:S(2)}) collective-permute-start(f32[16,32]{1,0:T(8,128)S(1)} %fusion.35), channel_id=1, source_target_pairs={{0,4},{4,0},{8,12},{12,8},{16,20},{20,16},{24,28},{28,24},{32,36},... | collective-permute-start | bytes 6152 | tf_op jit(solution)/shard_map/ppermute | solution.py:19
  73.4 1.5 collective-permute-done.12
  74.9 3.2 %collective-permute-start.13 = (f32[16,64]{1,0:T(8,128)S(1)}, f32[16,64]{1,0:T(8,128)S(1)}, u32[]{:S(2)}, u32[]{:S(2)}) collective-permute-start(f32[16,64]{1,0:T(8,128)S(1)} %maximum_select_fusion.5), channel_id=1, source_target_pairs={{0,64},{64,0},{128,192},{192,128},{256,320},{320,256},{384,448},{4... | collective-permute-start | bytes 12296 | tf_op jit(solution)/shard_map/ppermute | solution.py:19
  78.2 0.8 collective-permute-done.13
  79.0 5.7 %collective-permute-start.14 = (f32[16,128]{1,0:T(8,128)S(1)}, f32[16,128]{1,0:T(8,128)S(1)}, u32[]{:S(2)}, u32[]{:S(2)}) collective-permute-start(f32[16,128]{1,0:T(8,128)S(1)} %maximum_select_fusion.6), channel_id=1, source_target_pairs={{0,8},{4,12},{8,16},{12,20},{16,24},{20,28},{24,32},{28,36},{32,40... | collective-permute-start | bytes 24584 | tf_op jit(solution)/shard_map/ppermute | solution.py:15
  84.8 1.3 collective-permute-start.15
  86.1 4.9 %collective-permute-done.15 = f32[16,128]{1,0:T(8,128)S(1)} collective-permute-done((f32[16,128]{1,0:T(8,128)S(1)}, f32[16,128]{1,0:T(8,128)S(1)}, u32[]{:S(2)}, u32[]{:S(2)}) %collective-permute-start.15) | collective-permute-done | bytes 8224 | tf_op jit(solution)/shard_map/ppermute | solution.py:15
  91.1 3.1 %collective-permute-start.16 = (f32[3,16,128]{2,1,0:T(8,128)S(1)}, f32[3,16,128]{2,1,0:T(8,128)S(1)}, u32[]{:S(2)}, u32[]{:S(2)}) collective-permute-start(f32[3,16,128]{2,1,0:T(8,128)S(1)} %get-tuple-element.16), channel_id=1, source_target_pairs={{0,128},{64,192},{128,256},{192,320},{256,384},{320,448},{1,129},{... | collective-permute-start | bytes 73736 | tf_op jit(solution)/shard_map/ppermute | solution.py:15
  94.2 1.3 collective-permute-start.17
  95.6 3.1 %collective-permute-done.17 = f32[3,16,128]{2,1,0:T(8,128)S(1)} collective-permute-done((f32[3,16,128]{2,1,0:T(8,128)S(1)}, f32[3,16,128]{2,1,0:T(8,128)S(1)}, u32[]{:S(2)}, u32[]{:S(2)}) %collective-permute-start.17) | collective-permute-done | bytes 24608 | tf_op jit(solution)/shard_map/ppermute | solution.py:15
  99.0 2.9 %collective-permute-start.18 = (f32[16,32]{1,0:T(8,128)S(1)}, f32[16,32]{1,0:T(8,128)S(1)}, u32[]{:S(2)}, u32[]{:S(2)}) collective-permute-start(f32[16,32]{1,0:T(8,128)S(1)} %fusion.4), channel_id=1, source_target_pairs={{0,4},{4,0},{8,12},{12,8},{16,20},{20,16},{24,28},{28,24},{32,36},... | collective-permute-start | bytes 6152 | tf_op jit(solution)/shard_map/ppermute | solution.py:19
  102.0 1.4 collective-permute-done.18
  103.5 6.0 %collective-permute-start.19 = (f32[16,64]{1,0:T(8,128)S(1)}, f32[16,64]{1,0:T(8,128)S(1)}, u32[]{:S(2)}, u32[]{:S(2)}) collective-permute-start(f32[16,64]{1,0:T(8,128)S(1)} %maximum_select_fusion.8), channel_id=1, source_target_pairs={{0,64},{64,0},{128,192},{192,128},{256,320},{320,256},{384,448},{4... | collective-permute-start | bytes 12296 | tf_op jit(solution)/shard_map/ppermute | solution.py:19
  109.5 3.2 %sort.46 = (s32[256]{0:T(256)}, s32[256]{0:T(256)S(1)}) sort(s32[256]{0:T(256)S(1)} %bitcast.202, s32[256]{0:T(256)S(1)} %iota.15), dimensions={0}, to_apply=%region_1.3 | sort | flops 2048 | bytes 4096 | tf_op jit(solution)/shard_map/jit(argsort)/sort | solution.py:35
  112.9 2.9 %collective-permute-start.20 = (f32[16,32]{1,0:T(8,128)S(1)}, f32[16,32]{1,0:T(8,128)S(1)}, u32[]{:S(2)}, u32[]{:S(2)}) collective-permute-start(f32[16,32]{1,0:T(8,128)S(1)} %fusion.33), channel_id=1, source_target_pairs={{0,4},{4,0},{8,12},{12,8},{16,20},{20,16},{24,28},{28,24},{32,36},... | collective-permute-start | bytes 6152 | tf_op jit(solution)/shard_map/ppermute | solution.py:19
  115.8 1.5 collective-permute-done.20
  117.4 3.1 %collective-permute-start.21 = (f32[16,64]{1,0:T(8,128)S(1)}, f32[16,64]{1,0:T(8,128)S(1)}, u32[]{:S(2)}, u32[]{:S(2)}) collective-permute-start(f32[16,64]{1,0:T(8,128)S(1)} %maximum_select_fusion.11), channel_id=1, source_target_pairs={{0,64},{64,0},{128,192},{192,128},{256,320},{320,256},{384,448},{4... | collective-permute-start | bytes 12296 | tf_op jit(solution)/shard_map/ppermute | solution.py:19
  120.5 0.8 collective-permute-done.21
  121.3 5.7 %collective-permute-start.22 = (f32[16,128]{1,0:T(8,128)S(1)}, f32[16,128]{1,0:T(8,128)S(1)}, u32[]{:S(2)}, u32[]{:S(2)}) collective-permute-start(f32[16,128]{1,0:T(8,128)S(1)} %maximum_select_fusion.12), channel_id=1, source_target_pairs={{0,8},{4,12},{8,16},{12,20},{16,24},{20,28},{24,32},{28,36},{32,40... | collective-permute-start | bytes 24584 | tf_op jit(solution)/shard_map/ppermute | solution.py:15
  127.1 1.3 collective-permute-start.23
  128.5 4.1 %collective-permute-done.23 = f32[16,128]{1,0:T(8,128)S(1)} collective-permute-done((f32[16,128]{1,0:T(8,128)S(1)}, f32[16,128]{1,0:T(8,128)S(1)}, u32[]{:S(2)}, u32[]{:S(2)}) %collective-permute-start.23) | collective-permute-done | bytes 8224 | tf_op jit(solution)/shard_map/ppermute | solution.py:15
  132.6 3.0 %collective-permute-start.24 = (f32[3,16,128]{2,1,0:T(8,128)S(1)}, f32[3,16,128]{2,1,0:T(8,128)S(1)}, u32[]{:S(2)}, u32[]{:S(2)}) collective-permute-start(f32[3,16,128]{2,1,0:T(8,128)S(1)} %get-tuple-element.14), channel_id=1, source_target_pairs={{0,128},{64,192},{128,256},{192,320},{256,384},{320,448},{1,129},{... | collective-permute-start | bytes 73736 | tf_op jit(solution)/shard_map/ppermute | solution.py:15
  135.6 1.3 collective-permute-start.25
  137.1 3.1 %collective-permute-done.25 = f32[3,16,128]{2,1,0:T(8,128)S(1)} collective-permute-done((f32[3,16,128]{2,1,0:T(8,128)S(1)}, f32[3,16,128]{2,1,0:T(8,128)S(1)}, u32[]{:S(2)}, u32[]{:S(2)}) %collective-permute-start.25) | collective-permute-done | bytes 24608 | tf_op jit(solution)/shard_map/ppermute | solution.py:15
  140.5 2.9 %collective-permute-start.26 = (f32[16,32]{1,0:T(8,128)S(1)}, f32[16,32]{1,0:T(8,128)S(1)}, u32[]{:S(2)}, u32[]{:S(2)}) collective-permute-start(f32[16,32]{1,0:T(8,128)S(1)} %fusion.3), channel_id=1, source_target_pairs={{0,4},{4,0},{8,12},{12,8},{16,20},{20,16},{24,28},{28,24},{32,36},... | collective-permute-start | bytes 6152 | tf_op jit(solution)/shard_map/ppermute | solution.py:19
  143.4 1.4 collective-permute-done.26
  144.9 6.0 %collective-permute-start.27 = (f32[16,64]{1,0:T(8,128)S(1)}, f32[16,64]{1,0:T(8,128)S(1)}, u32[]{:S(2)}, u32[]{:S(2)}) collective-permute-start(f32[16,64]{1,0:T(8,128)S(1)} %maximum_select_fusion.14), channel_id=1, source_target_pairs={{0,64},{64,0},{128,192},{192,128},{256,320},{320,256},{384,448},{4... | collective-permute-start | bytes 12296 | tf_op jit(solution)/shard_map/ppermute | solution.py:19
  151.0 0.8 collective-permute-done.27
  152.8 5.7 %collective-permute-start.28 = (f32[16,128]{1,0:T(8,128)S(1)}, f32[16,128]{1,0:T(8,128)S(1)}, u32[]{:S(2)}, u32[]{:S(2)}) collective-permute-start(f32[16,128]{1,0:T(8,128)S(1)} %constant_dynamic-slice_fusion.1), channel_id=1, source_target_pairs={{0,8},{4,12},{8,16},{12,20},{16,24},{20,28},{24,32},{28,36},{32,40... | collective-permute-start | bytes 24584 | tf_op jit(solution)/shard_map/ppermute | solution.py:15
  158.5 1.3 collective-permute-start.29
  159.8 4.0 %collective-permute-done.29 = f32[16,128]{1,0:T(8,128)S(1)} collective-permute-done((f32[16,128]{1,0:T(8,128)S(1)}, f32[16,128]{1,0:T(8,128)S(1)}, u32[]{:S(2)}, u32[]{:S(2)}) %collective-permute-start.29) | collective-permute-done | bytes 8224 | tf_op jit(solution)/shard_map/ppermute | solution.py:15
  163.8 4.5 %collective-permute-start.30 = (f32[3,16,128]{2,1,0:T(8,128)S(1)}, f32[3,16,128]{2,1,0:T(8,128)S(1)}, u32[]{:S(2)}, u32[]{:S(2)}) collective-permute-start(f32[3,16,128]{2,1,0:T(8,128)S(1)} %get-tuple-element.12), channel_id=1, source_target_pairs={{0,64},{64,128},{128,192},{192,256},{256,320},{320,384},{384,448},... | collective-permute-start | bytes 73736 | tf_op jit(solution)/shard_map/ppermute | solution.py:15
  168.3 1.9 collective-permute-start.31
  170.2 3.2 %collective-permute-done.31 = f32[3,16,128]{2,1,0:T(8,128)S(1)} collective-permute-done((f32[3,16,128]{2,1,0:T(8,128)S(1)}, f32[3,16,128]{2,1,0:T(8,128)S(1)}, u32[]{:S(2)}, u32[]{:S(2)}) %collective-permute-start.31) | collective-permute-done | bytes 24608 | tf_op jit(solution)/shard_map/ppermute | solution.py:15
  174.3 3.1 %collective-permute-start.32 = (f32[16,64]{1,0:T(8,128)S(1)}, f32[16,64]{1,0:T(8,128)S(1)}, u32[]{:S(2)}, u32[]{:S(2)}) collective-permute-start(f32[16,64]{1,0:T(8,128)S(1)} %fusion.2), channel_id=1, source_target_pairs={{0,4},{4,0},{8,12},{12,8},{16,20},{20,16},{24,28},{28,24},{32,36},... | collective-permute-start | bytes 12296 | tf_op jit(solution)/shard_map/ppermute | solution.py:19
  177.5 1.3 dynamic-slice
  179.6 0.7 gather_fusion.4
  180.4 2.4 %collective-permute-start.33 = (f32[16,128]{1,0:T(8,128)S(1)}, f32[16,128]{1,0:T(8,128)S(1)}, u32[]{:S(2)}, u32[]{:S(2)}) collective-permute-start(f32[16,128]{1,0:T(8,128)S(1)} %constant_dynamic-slice_fusion), channel_id=1, source_target_pairs={{0,4},{4,8},{8,12},{12,16},{16,20},{20,24},{24,28},{28,32},{32,36}... | collective-permute-start | bytes 24584 | tf_op jit(solution)/shard_map/ppermute | solution.py:15
  182.8 1.3 collective-permute-start.34
  184.2 3.2 %collective-permute-done.34 = f32[16,128]{1,0:T(8,128)S(1)} collective-permute-done((f32[16,128]{1,0:T(8,128)S(1)}, f32[16,128]{1,0:T(8,128)S(1)}, u32[]{:S(2)}, u32[]{:S(2)}) %collective-permute-start.34) | collective-permute-done | bytes 8224 | tf_op jit(solution)/shard_map/ppermute | solution.py:15
  187.4 4.3 %collective-permute-start.35 = (f32[3,16,128]{2,1,0:T(8,128)S(1)}, f32[3,16,128]{2,1,0:T(8,128)S(1)}, u32[]{:S(2)}, u32[]{:S(2)}) collective-permute-start(f32[3,16,128]{2,1,0:T(8,128)S(1)} %get-tuple-element.10), channel_id=1, source_target_pairs={{0,64},{64,128},{128,192},{192,256},{256,320},{320,384},{384,448},... | collective-permute-start | bytes 73736 | tf_op jit(solution)/shard_map/ppermute | solution.py:15
  191.7 1.9 collective-permute-start.36
  193.9 3.0 %collective-permute-done.36 = f32[3,16,128]{2,1,0:T(8,128)S(1)} collective-permute-done((f32[3,16,128]{2,1,0:T(8,128)S(1)}, f32[3,16,128]{2,1,0:T(8,128)S(1)}, u32[]{:S(2)}, u32[]{:S(2)}) %collective-permute-start.36) | collective-permute-done | bytes 24608 | tf_op jit(solution)/shard_map/ppermute | solution.py:15
  200.6 8.7 %all-reduce = f32[1,1,16]{2,1,0:T(1,128)S(1)} all-reduce(f32[1,1,16]{2,1,0:T(1,128)S(1)} %convolution_bitcast_fusion.6), channel_id=2, replica_groups=mesh['bx'=8,'by'=16,'rhs'=4] {'rhs'}, use_global_device_ids=true, to_apply=%region_4.6.clone | all-reduce | flops 16 | bytes 128
  (163 shorter events, 16.7 us)
Async XLA Ops:
  0.6 26.0 %copy-start = (f32[1,1,9,128,128]{4,3,2,1,0:T(8,128)S(1)}, f32[1,1,9,128,128]{4,3,2,1,0:T(8,128)}, u32[]{:S(2)}) copy-start(f32[1,1,9,128,128]{4,3,2,1,0:T(8,128)} %param.36) | copy-start | bytes 1769476
  0.6 4.6 %copy-start.15 = (f32[1,1,16,256]{3,2,1,0:T(8,128)S(1)}, f32[1,1,16,256]{3,2,1,0:T(8,128)}, u32[]{:S(2)}) copy-start(f32[1,1,16,256]{3,2,1,0:T(8,128)} %param.27) | copy-start | bytes 49156
  7.3 0.7 copy-start.22
  7.3 0.7 copy-start.23
  7.3 0.9 copy-start.9
  7.4 7.3 %copy-start.10 = (f32[1,1,128,128]{3,2,1,0:T(8,128)S(1)}, f32[1,1,128,128]{3,2,1,0:T(8,128)}, u32[]{:S(2)}) copy-start(f32[1,1,128,128]{3,2,1,0:T(8,128)} %param.34) | copy-start | bytes 196612
  8.3 6.5 %collective-permute-start.1 = (f32[16,128]{1,0:T(8,128)S(1)}, f32[16,128]{1,0:T(8,128)S(1)}, u32[]{:S(2)}, u32[]{:S(2)}) collective-permute-start(f32[16,128]{1,0:T(8,128)S(1)} %fusion.21), channel_id=1, source_target_pairs={{4,0},{8,4},{12,8},{16,12},{20,16},{24,20},{28,24},{32,28},{36,32}... | collective-permute-start | bytes 24584 | tf_op jit(solution)/shard_map/ppermute | solution.py:15
  9.6 5.8 %collective-permute-start = (f32[16,128]{1,0:T(8,128)S(1)}, f32[16,128]{1,0:T(8,128)S(1)}, u32[]{:S(2)}, u32[]{:S(2)}) collective-permute-start(f32[16,128]{1,0:T(8,128)S(1)} %fusion.21), channel_id=1, source_target_pairs={{0,4},{4,8},{8,12},{12,16},{16,20},{20,24},{24,28},{28,32},{32,36}... | collective-permute-start | bytes 24584 | tf_op jit(solution)/shard_map/ppermute | solution.py:15
  15.4 10.3 %copy-start.25 = (s32[1,1,9]{2,1,0:T(1,128)S(1)}, s32[1,1,9]{2,1,0:T(1,128)}, u32[]{:S(2)}) copy-start(s32[1,1,9]{2,1,0:T(1,128)} %param.33) | copy-start | bytes 112
  15.4 10.5 %collective-permute-start.2 = (f32[3,16,128]{2,1,0:T(8,128)S(1)}, f32[3,16,128]{2,1,0:T(8,128)S(1)}, u32[]{:S(2)}, u32[]{:S(2)}) collective-permute-start(f32[3,16,128]{2,1,0:T(8,128)S(1)} %get-tuple-element.20), channel_id=1, source_target_pairs={{0,64},{64,128},{128,192},{192,256},{256,320},{320,384},{384,448},... | collective-permute-start | bytes 73736 | tf_op jit(solution)/shard_map/ppermute | solution.py:15
  20.2 6.4 %collective-permute-start.3 = (f32[3,16,128]{2,1,0:T(8,128)S(1)}, f32[3,16,128]{2,1,0:T(8,128)S(1)}, u32[]{:S(2)}, u32[]{:S(2)}) collective-permute-start(f32[3,16,128]{2,1,0:T(8,128)S(1)} %get-tuple-element.20), channel_id=1, source_target_pairs={{64,0},{128,64},{192,128},{256,192},{320,256},{384,320},{448,384},... | collective-permute-start | bytes 73736 | tf_op jit(solution)/shard_map/ppermute | solution.py:15
  27.1 4.9 %collective-permute-start.4 = (f32[16,128]{1,0:T(8,128)S(1)}, f32[16,128]{1,0:T(8,128)S(1)}, u32[]{:S(2)}, u32[]{:S(2)}) collective-permute-start(f32[16,128]{1,0:T(8,128)S(1)} %fusion.6), channel_id=1, source_target_pairs={{0,4},{4,0},{8,12},{12,8},{16,20},{20,16},{24,28},{28,24},{32,36},... | collective-permute-start | bytes 24584 | tf_op jit(solution)/shard_map/ppermute | solution.py:19
  32.1 0.8 copy-start.13
  32.1 4.4 %copy-start.21 = (s32[1,1,256]{2,1,0:T(1,128)S(1)}, s32[1,1,256]{2,1,0:T(1,128)}, u32[]{:S(2)}) copy-start(s32[1,1,256]{2,1,0:T(1,128)} %param.45) | copy-start | bytes 3076
  32.9 27.4 %copy-start.3 = (f32[1,1,9,128,64]{3,4,2,1,0:T(8,128)S(1)}, f32[1,1,9,128,64]{3,4,2,1,0:T(8,128)}, u32[]{:S(2)}) copy-start(f32[1,1,9,128,64]{3,4,2,1,0:T(8,128)} %param.42) | copy-start | bytes 884740
  33.1 6.6 %collective-permute-start.5 = (f32[16,64]{1,0:T(8,128)S(1)}, f32[16,64]{1,0:T(8,128)S(1)}, u32[]{:S(2)}, u32[]{:S(2)}) collective-permute-start(f32[16,64]{1,0:T(8,128)S(1)} %fusion.28), channel_id=1, source_target_pairs={{0,4},{4,0},{8,12},{12,8},{16,20},{20,16},{24,28},{28,24},{32,36},... | collective-permute-start | bytes 12296 | tf_op jit(solution)/shard_map/ppermute | solution.py:19
  39.8 5.9 %collective-permute-start.6 = (f32[16,128]{1,0:T(8,128)S(1)}, f32[16,128]{1,0:T(8,128)S(1)}, u32[]{:S(2)}, u32[]{:S(2)}) collective-permute-start(f32[16,128]{1,0:T(8,128)S(1)} %maximum_select_fusion.2), channel_id=1, source_target_pairs={{0,8},{4,12},{8,16},{12,20},{16,24},{20,28},{24,32},{28,36},{32,40... | collective-permute-start | bytes 24584 | tf_op jit(solution)/shard_map/ppermute | solution.py:15
  44.3 6.4 %collective-permute-start.7 = (f32[16,128]{1,0:T(8,128)S(1)}, f32[16,128]{1,0:T(8,128)S(1)}, u32[]{:S(2)}, u32[]{:S(2)}) collective-permute-start(f32[16,128]{1,0:T(8,128)S(1)} %maximum_select_fusion.2), channel_id=1, source_target_pairs={{8,0},{12,4},{16,8},{20,12},{24,16},{28,20},{32,24},{36,28},{40,32... | collective-permute-start | bytes 24584 | tf_op jit(solution)/shard_map/ppermute | solution.py:15
  50.7 6.3 %collective-permute-start.8 = (f32[3,16,128]{2,1,0:T(8,128)S(1)}, f32[3,16,128]{2,1,0:T(8,128)S(1)}, u32[]{:S(2)}, u32[]{:S(2)}) collective-permute-start(f32[3,16,128]{2,1,0:T(8,128)S(1)} %get-tuple-element.18), channel_id=1, source_target_pairs={{0,64},{64,128},{128,192},{192,256},{256,320},{320,384},{384,448},... | collective-permute-start | bytes 73736 | tf_op jit(solution)/shard_map/ppermute | solution.py:15
  55.1 5.1 %collective-permute-start.9 = (f32[3,16,128]{2,1,0:T(8,128)S(1)}, f32[3,16,128]{2,1,0:T(8,128)S(1)}, u32[]{:S(2)}, u32[]{:S(2)}) collective-permute-start(f32[3,16,128]{2,1,0:T(8,128)S(1)} %get-tuple-element.18), channel_id=1, source_target_pairs={{64,0},{128,64},{192,128},{256,192},{320,256},{384,320},{448,384},... | collective-permute-start | bytes 73736 | tf_op jit(solution)/shard_map/ppermute | solution.py:15
  60.3 0.8 copy-start.12
  61.1 4.4 %collective-permute-start.10 = (f32[16,64]{1,0:T(8,128)S(1)}, f32[16,64]{1,0:T(8,128)S(1)}, u32[]{:S(2)}, u32[]{:S(2)}) collective-permute-start(f32[16,64]{1,0:T(8,128)S(1)} %fusion.5), channel_id=1, source_target_pairs={{0,4},{4,0},{8,12},{12,8},{16,20},{20,16},{24,28},{28,24},{32,36},... | collective-permute-start | bytes 12296 | tf_op jit(solution)/shard_map/ppermute | solution.py:19
  65.7 3.1 %collective-permute-start.11 = (f32[16,128]{1,0:T(8,128)S(1)}, f32[16,128]{1,0:T(8,128)S(1)}, u32[]{:S(2)}, u32[]{:S(2)}) collective-permute-start(f32[16,128]{1,0:T(8,128)S(1)} %maximum_select_fusion.4), channel_id=1, source_target_pairs={{0,64},{64,0},{128,192},{192,128},{256,320},{320,256},{384,448},{4... | collective-permute-start | bytes 24584 | tf_op jit(solution)/shard_map/ppermute | solution.py:19
  69.6 0.7 copy-start.17
  70.5 4.4 %collective-permute-start.12 = (f32[16,32]{1,0:T(8,128)S(1)}, f32[16,32]{1,0:T(8,128)S(1)}, u32[]{:S(2)}, u32[]{:S(2)}) collective-permute-start(f32[16,32]{1,0:T(8,128)S(1)} %fusion.35), channel_id=1, source_target_pairs={{0,4},{4,0},{8,12},{12,8},{16,20},{20,16},{24,28},{28,24},{32,36},... | collective-permute-start | bytes 6152 | tf_op jit(solution)/shard_map/ppermute | solution.py:19
  74.9 4.0 %collective-permute-start.13 = (f32[16,64]{1,0:T(8,128)S(1)}, f32[16,64]{1,0:T(8,128)S(1)}, u32[]{:S(2)}, u32[]{:S(2)}) collective-permute-start(f32[16,64]{1,0:T(8,128)S(1)} %maximum_select_fusion.5), channel_id=1, source_target_pairs={{0,64},{64,0},{128,192},{192,128},{256,320},{320,256},{384,448},{4... | collective-permute-start | bytes 12296 | tf_op jit(solution)/shard_map/ppermute | solution.py:19
  79.0 16.5 %copy-start.18 = (f32[1,1,128,32]{2,3,1,0:T(8,128)S(1)}, f32[1,1,128,32]{2,3,1,0:T(8,128)}, u32[]{:S(2)}) copy-start(f32[1,1,128,32]{2,3,1,0:T(8,128)} %param.46) | copy-start | bytes 49156
  79.0 7.1 %collective-permute-start.14 = (f32[16,128]{1,0:T(8,128)S(1)}, f32[16,128]{1,0:T(8,128)S(1)}, u32[]{:S(2)}, u32[]{:S(2)}) collective-permute-start(f32[16,128]{1,0:T(8,128)S(1)} %maximum_select_fusion.6), channel_id=1, source_target_pairs={{0,8},{4,12},{8,16},{12,20},{16,24},{20,28},{24,32},{28,36},{32,40... | collective-permute-start | bytes 24584 | tf_op jit(solution)/shard_map/ppermute | solution.py:15
  84.8 6.3 %collective-permute-start.15 = (f32[16,128]{1,0:T(8,128)S(1)}, f32[16,128]{1,0:T(8,128)S(1)}, u32[]{:S(2)}, u32[]{:S(2)}) collective-permute-start(f32[16,128]{1,0:T(8,128)S(1)} %maximum_select_fusion.6), channel_id=1, source_target_pairs={{8,0},{12,4},{16,8},{20,12},{24,16},{28,20},{32,24},{36,28},{40,32... | collective-permute-start | bytes 24584 | tf_op jit(solution)/shard_map/ppermute | solution.py:15
  86.1 12.7 %copy-start.6 = (f32[1,1,9,128,32]{3,4,2,1,0:T(8,128)S(1)}, f32[1,1,9,128,32]{3,4,2,1,0:T(8,128)}, u32[]{:S(2)}) copy-start(f32[1,1,9,128,32]{3,4,2,1,0:T(8,128)} %param.48) | copy-start | bytes 442372
  91.1 4.5 %collective-permute-start.16 = (f32[3,16,128]{2,1,0:T(8,128)S(1)}, f32[3,16,128]{2,1,0:T(8,128)S(1)}, u32[]{:S(2)}, u32[]{:S(2)}) collective-permute-start(f32[3,16,128]{2,1,0:T(8,128)S(1)} %get-tuple-element.16), channel_id=1, source_target_pairs={{0,128},{64,192},{128,256},{192,320},{256,384},{320,448},{1,129},{... | collective-permute-start | bytes 73736 | tf_op jit(solution)/shard_map/ppermute | solution.py:15
  94.2 4.6 %collective-permute-start.17 = (f32[3,16,128]{2,1,0:T(8,128)S(1)}, f32[3,16,128]{2,1,0:T(8,128)S(1)}, u32[]{:S(2)}, u32[]{:S(2)}) collective-permute-start(f32[3,16,128]{2,1,0:T(8,128)S(1)} %get-tuple-element.16), channel_id=1, source_target_pairs={{128,0},{192,64},{256,128},{320,192},{384,256},{448,320},{129,1},{... | collective-permute-start | bytes 73736 | tf_op jit(solution)/shard_map/ppermute | solution.py:15
  99.0 13.7 %copy-start.20 = (f32[1,1,128,32]{2,3,1,0:T(8,128)S(1)}, f32[1,1,128,32]{2,3,1,0:T(8,128)}, u32[]{:S(2)}) copy-start(f32[1,1,128,32]{2,3,1,0:T(8,128)} %param.51) | copy-start | bytes 49156
  99.0 4.4 %collective-permute-start.18 = (f32[16,32]{1,0:T(8,128)S(1)}, f32[16,32]{1,0:T(8,128)S(1)}, u32[]{:S(2)}, u32[]{:S(2)}) collective-permute-start(f32[16,32]{1,0:T(8,128)S(1)} %fusion.4), channel_id=1, source_target_pairs={{0,4},{4,0},{8,12},{12,8},{16,20},{20,16},{24,28},{28,24},{32,36},... | collective-permute-start | bytes 6152 | tf_op jit(solution)/shard_map/ppermute | solution.py:19
  103.5 9.2 %collective-permute-start.19 = (f32[16,64]{1,0:T(8,128)S(1)}, f32[16,64]{1,0:T(8,128)S(1)}, u32[]{:S(2)}, u32[]{:S(2)}) collective-permute-start(f32[16,64]{1,0:T(8,128)S(1)} %maximum_select_fusion.8), channel_id=1, source_target_pairs={{0,64},{64,0},{128,192},{192,128},{256,320},{320,256},{384,448},{4... | collective-permute-start | bytes 12296 | tf_op jit(solution)/shard_map/ppermute | solution.py:19
  112.9 4.4 %collective-permute-start.20 = (f32[16,32]{1,0:T(8,128)S(1)}, f32[16,32]{1,0:T(8,128)S(1)}, u32[]{:S(2)}, u32[]{:S(2)}) collective-permute-start(f32[16,32]{1,0:T(8,128)S(1)} %fusion.33), channel_id=1, source_target_pairs={{0,4},{4,0},{8,12},{12,8},{16,20},{20,16},{24,28},{28,24},{32,36},... | collective-permute-start | bytes 6152 | tf_op jit(solution)/shard_map/ppermute | solution.py:19
  117.4 3.9 %collective-permute-start.21 = (f32[16,64]{1,0:T(8,128)S(1)}, f32[16,64]{1,0:T(8,128)S(1)}, u32[]{:S(2)}, u32[]{:S(2)}) collective-permute-start(f32[16,64]{1,0:T(8,128)S(1)} %maximum_select_fusion.11), channel_id=1, source_target_pairs={{0,64},{64,0},{128,192},{192,128},{256,320},{320,256},{384,448},{4... | collective-permute-start | bytes 12296 | tf_op jit(solution)/shard_map/ppermute | solution.py:19
  121.2 15.7 %copy-start.19 = (f32[1,1,128,32]{2,3,1,0:T(8,128)S(1)}, f32[1,1,128,32]{2,3,1,0:T(8,128)}, u32[]{:S(2)}) copy-start(f32[1,1,128,32]{2,3,1,0:T(8,128)} %param.49) | copy-start | bytes 49156
  121.3 7.1 %collective-permute-start.22 = (f32[16,128]{1,0:T(8,128)S(1)}, f32[16,128]{1,0:T(8,128)S(1)}, u32[]{:S(2)}, u32[]{:S(2)}) collective-permute-start(f32[16,128]{1,0:T(8,128)S(1)} %maximum_select_fusion.12), channel_id=1, source_target_pairs={{0,8},{4,12},{8,16},{12,20},{16,24},{20,28},{24,32},{28,36},{32,40... | collective-permute-start | bytes 24584 | tf_op jit(solution)/shard_map/ppermute | solution.py:15
  127.1 5.5 %collective-permute-start.23 = (f32[16,128]{1,0:T(8,128)S(1)}, f32[16,128]{1,0:T(8,128)S(1)}, u32[]{:S(2)}, u32[]{:S(2)}) collective-permute-start(f32[16,128]{1,0:T(8,128)S(1)} %maximum_select_fusion.12), channel_id=1, source_target_pairs={{8,0},{12,4},{16,8},{20,12},{24,16},{28,20},{32,24},{36,28},{40,32... | collective-permute-start | bytes 24584 | tf_op jit(solution)/shard_map/ppermute | solution.py:15
  128.4 11.8 %copy-start.7 = (f32[1,1,9,128,32]{3,4,2,1,0:T(8,128)S(1)}, f32[1,1,9,128,32]{3,4,2,1,0:T(8,128)}, u32[]{:S(2)}) copy-start(f32[1,1,9,128,32]{3,4,2,1,0:T(8,128)} %param.50) | copy-start | bytes 442372
  132.6 4.5 %collective-permute-start.24 = (f32[3,16,128]{2,1,0:T(8,128)S(1)}, f32[3,16,128]{2,1,0:T(8,128)S(1)}, u32[]{:S(2)}, u32[]{:S(2)}) collective-permute-start(f32[3,16,128]{2,1,0:T(8,128)S(1)} %get-tuple-element.14), channel_id=1, source_target_pairs={{0,128},{64,192},{128,256},{192,320},{256,384},{320,448},{1,129},{... | collective-permute-start | bytes 73736 | tf_op jit(solution)/shard_map/ppermute | solution.py:15
  135.6 4.6 %collective-permute-start.25 = (f32[3,16,128]{2,1,0:T(8,128)S(1)}, f32[3,16,128]{2,1,0:T(8,128)S(1)}, u32[]{:S(2)}, u32[]{:S(2)}) collective-permute-start(f32[3,16,128]{2,1,0:T(8,128)S(1)} %get-tuple-element.14), channel_id=1, source_target_pairs={{128,0},{192,64},{256,128},{320,192},{384,256},{448,320},{129,1},{... | collective-permute-start | bytes 73736 | tf_op jit(solution)/shard_map/ppermute | solution.py:15
  140.5 4.4 %collective-permute-start.26 = (f32[16,32]{1,0:T(8,128)S(1)}, f32[16,32]{1,0:T(8,128)S(1)}, u32[]{:S(2)}, u32[]{:S(2)}) collective-permute-start(f32[16,32]{1,0:T(8,128)S(1)} %fusion.3), channel_id=1, source_target_pairs={{0,4},{4,0},{8,12},{12,8},{16,20},{20,16},{24,28},{28,24},{32,36},... | collective-permute-start | bytes 6152 | tf_op jit(solution)/shard_map/ppermute | solution.py:19
  144.9 6.8 %collective-permute-start.27 = (f32[16,64]{1,0:T(8,128)S(1)}, f32[16,64]{1,0:T(8,128)S(1)}, u32[]{:S(2)}, u32[]{:S(2)}) collective-permute-start(f32[16,64]{1,0:T(8,128)S(1)} %maximum_select_fusion.14), channel_id=1, source_target_pairs={{0,64},{64,0},{128,192},{192,128},{256,320},{320,256},{384,448},{4... | collective-permute-start | bytes 12296 | tf_op jit(solution)/shard_map/ppermute | solution.py:19
  152.0 21.5 %copy-start.4 = (f32[1,1,9,128,64]{3,4,2,1,0:T(8,128)S(1)}, f32[1,1,9,128,64]{3,4,2,1,0:T(8,128)}, u32[]{:S(2)}) copy-start(f32[1,1,9,128,64]{3,4,2,1,0:T(8,128)} %param.44) | copy-start | bytes 884740
  152.8 7.0 %collective-permute-start.28 = (f32[16,128]{1,0:T(8,128)S(1)}, f32[16,128]{1,0:T(8,128)S(1)}, u32[]{:S(2)}, u32[]{:S(2)}) collective-permute-start(f32[16,128]{1,0:T(8,128)S(1)} %constant_dynamic-slice_fusion.1), channel_id=1, source_target_pairs={{0,8},{4,12},{8,16},{12,20},{16,24},{20,28},{24,32},{28,36},{32,40... | collective-permute-start | bytes 24584 | tf_op jit(solution)/shard_map/ppermute | solution.py:15
  158.5 5.3 %collective-permute-start.29 = (f32[16,128]{1,0:T(8,128)S(1)}, f32[16,128]{1,0:T(8,128)S(1)}, u32[]{:S(2)}, u32[]{:S(2)}) collective-permute-start(f32[16,128]{1,0:T(8,128)S(1)} %constant_dynamic-slice_fusion.1), channel_id=1, source_target_pairs={{8,0},{12,4},{16,8},{20,12},{24,16},{28,20},{32,24},{36,28},{40,32... | collective-permute-start | bytes 24584 | tf_op jit(solution)/shard_map/ppermute | solution.py:15
  163.8 6.4 %collective-permute-start.30 = (f32[3,16,128]{2,1,0:T(8,128)S(1)}, f32[3,16,128]{2,1,0:T(8,128)S(1)}, u32[]{:S(2)}, u32[]{:S(2)}) collective-permute-start(f32[3,16,128]{2,1,0:T(8,128)S(1)} %get-tuple-element.12), channel_id=1, source_target_pairs={{0,64},{64,128},{128,192},{192,256},{256,320},{320,384},{384,448},... | collective-permute-start | bytes 73736 | tf_op jit(solution)/shard_map/ppermute | solution.py:15
  168.3 5.1 %collective-permute-start.31 = (f32[3,16,128]{2,1,0:T(8,128)S(1)}, f32[3,16,128]{2,1,0:T(8,128)S(1)}, u32[]{:S(2)}, u32[]{:S(2)}) collective-permute-start(f32[3,16,128]{2,1,0:T(8,128)S(1)} %get-tuple-element.12), channel_id=1, source_target_pairs={{64,0},{128,64},{192,128},{256,192},{320,256},{384,320},{448,384},... | collective-permute-start | bytes 73736 | tf_op jit(solution)/shard_map/ppermute | solution.py:15
  173.4 0.8 copy-start.14
  174.2 22.8 %copy-start.2 = (f32[1,1,9,128,128]{4,3,2,1,0:T(8,128)S(1)}, f32[1,1,9,128,128]{4,3,2,1,0:T(8,128)}, u32[]{:S(2)}) copy-start(f32[1,1,9,128,128]{4,3,2,1,0:T(8,128)} %param.38) | copy-start | bytes 1769476
  174.3 5.1 %collective-permute-start.32 = (f32[16,64]{1,0:T(8,128)S(1)}, f32[16,64]{1,0:T(8,128)S(1)}, u32[]{:S(2)}, u32[]{:S(2)}) collective-permute-start(f32[16,64]{1,0:T(8,128)S(1)} %fusion.2), channel_id=1, source_target_pairs={{0,4},{4,0},{8,12},{12,8},{16,20},{20,16},{24,28},{28,24},{32,36},... | collective-permute-start | bytes 12296 | tf_op jit(solution)/shard_map/ppermute | solution.py:19
  180.4 13.3 %copy-start.11 = (f32[1,1,128,128]{3,2,1,0:T(8,128)S(1)}, f32[1,1,128,128]{3,2,1,0:T(8,128)}, u32[]{:S(2)}) copy-start(f32[1,1,128,128]{3,2,1,0:T(8,128)} %param.37) | copy-start | bytes 196612
  180.4 3.8 %collective-permute-start.33 = (f32[16,128]{1,0:T(8,128)S(1)}, f32[16,128]{1,0:T(8,128)S(1)}, u32[]{:S(2)}, u32[]{:S(2)}) collective-permute-start(f32[16,128]{1,0:T(8,128)S(1)} %constant_dynamic-slice_fusion), channel_id=1, source_target_pairs={{0,4},{4,8},{8,12},{12,16},{16,20},{20,24},{24,28},{28,32},{32,36}... | collective-permute-start | bytes 24584 | tf_op jit(solution)/shard_map/ppermute | solution.py:15
  182.8 4.6 %collective-permute-start.34 = (f32[16,128]{1,0:T(8,128)S(1)}, f32[16,128]{1,0:T(8,128)S(1)}, u32[]{:S(2)}, u32[]{:S(2)}) collective-permute-start(f32[16,128]{1,0:T(8,128)S(1)} %constant_dynamic-slice_fusion), channel_id=1, source_target_pairs={{4,0},{8,4},{12,8},{16,12},{20,16},{24,20},{28,24},{32,28},{36,32}... | collective-permute-start | bytes 24584 | tf_op jit(solution)/shard_map/ppermute | solution.py:15
  187.4 6.4 %collective-permute-start.35 = (f32[3,16,128]{2,1,0:T(8,128)S(1)}, f32[3,16,128]{2,1,0:T(8,128)S(1)}, u32[]{:S(2)}, u32[]{:S(2)}) collective-permute-start(f32[3,16,128]{2,1,0:T(8,128)S(1)} %get-tuple-element.10), channel_id=1, source_target_pairs={{0,64},{64,128},{128,192},{192,256},{256,320},{320,384},{384,448},... | collective-permute-start | bytes 73736 | tf_op jit(solution)/shard_map/ppermute | solution.py:15
  191.7 5.1 %collective-permute-start.36 = (f32[3,16,128]{2,1,0:T(8,128)S(1)}, f32[3,16,128]{2,1,0:T(8,128)S(1)}, u32[]{:S(2)}, u32[]{:S(2)}) collective-permute-start(f32[3,16,128]{2,1,0:T(8,128)S(1)} %get-tuple-element.10), channel_id=1, source_target_pairs={{64,0},{128,64},{192,128},{256,192},{320,256},{384,320},{448,384},... | collective-permute-start | bytes 73736 | tf_op jit(solution)/shard_map/ppermute | solution.py:15
  197.4 1.0 copy-start.1
  197.5 1.2 copy-start.5
  198.4 0.7 copy-start.16
  199.1 0.6 copy-start.8
  199.7 0.7 copy-start.24
where the time goes:
time: 212 us; the launch traced here: 210 us
  starting transfers between devices  120 us (57%)
  waiting for transfers between devices  50.2 us (24%)
  other arithmetic  12.3 us (6%)
  local copies, waits for them, and re-layouts  11 us (5%)
  blocking collectives  8.71 us (4%)
  matrix products  5.57 us (3%)
  between operations  2.21 us (1%)
    ppermute x24, starting transfers between devices, from_behind(): return lax.ppermute(shard, axis, pairs)  74.7 us
    ppermute x13, starting transfers between devices, swapped(): lax.ppermute(shard, axis, [(i, i ^ 1 << apart) for i in range(lax.axis_si...  45.3 us
    ppermute x24, waiting for transfers between devices, from_behind(): return lax.ppermute(shard, axis, pairs)  38.4 us
    ppermute x13, waiting for transfers between devices, swapped(): lax.ppermute(shard, axis, [(i, i ^ 1 << apart) for i in range(lax.axis_si...  11.8 us
    sort x3, other arithmetic, placed_cols(): return jnp.take(values, jnp.argsort(order), axis=1)  10.2 us
    unnamed x1, blocking collectives  8.71 us
    unnamed x54, local copies, waits for them, and re-layouts  5.67 us
  transfers between devices with their start and end apart: 37, of which 23 were waited for; matrix products, arithmetic and copies ran while one was open for 4% of the time, Pallas kernels for 0%

commit v1 on v0

v1 whole, which is shorter than its diff:
```python
import functools

import jax
import jax.numpy as jnp
from jax import lax
from jax.sharding import PartitionSpec as P

PANELS = 16
AXES = ("bx", "by", "rhs")
PRECISION = lax.Precision.HIGH


def dot(left, right):
    return lax.dot_general(
        left, right, (((1,), (0,)), ((), ())), precision=PRECISION, preferred_element_type=jnp.float32
    )


def dot_t(left, right):
    return lax.dot_general(
        left, right, (((1,), (1,)), ((), ())), precision=PRECISION, preferred_element_type=jnp.float32
    )


def lanes(*parts):
    return jnp.concatenate(parts, axis=-1)


def rows(*parts):
    return jnp.concatenate(parts, axis=0)


class Groups:
    def __init__(self, size_x, size_y, size_r):
        def place(i, j, r):
            return (i * size_y + j) * size_r + r

        every = [(i, j, r) for i in range(size_x) for j in range(size_y) for r in range(size_r)]
        self.sibling = [[place(i, j, r), place(i + 1, j, r)] for i, j, r in every if i % 2 == 0]
        self.diagonal = [[place(i, j, r), place(i + 1, j ^ 1, r)] for i, j, r in every if i % 2 == 0]
        self.shifted = []
        for j in range(1, size_y, 2):
            after = (j + 1) % size_y
            for r in range(size_r):
                for i in range(1, size_x - 1, 2):
                    self.shifted.append(
                        [place(i, j, r), place(i, after, r), place(i + 1, j, r), place(i + 1, after, r)]
                    )
                if r % 2 == 0:
                    for i in (0, size_x - 1):
                        self.shifted.append(
                            [place(i, j, r), place(i, after, r), place(i, j, r + 1), place(i, after, r + 1)]
                        )


def on_device(
    groups,
    rhs_nodes,
    forward,
    leaf_map,
    derivative,
    node_panel,
    order_one,
    near_one,
    interp_one,
    solve_one,
    couple_one,
    back_one,
    spread_one,
    order_two,
    interp_two,
    solve_two,
    couple_two,
    back_two,
    spread_two,
    order_three,
    interp_three,
    solve_three,
    couple_three,
    back_three,
    spread_three,
    top_three,
):
    skel = interp_one.shape[-1]
    half, quarter = skel // 2, skel // 4
    size_x, size_y = lax.axis_size("bx"), lax.axis_size("by")
    place_x, place_y, place_r = (lax.axis_index(axis) for axis in AXES)
    upper_x, upper_y = place_x % 2 == 1, place_y % 2 == 1
    same = upper_x == upper_y
    edge_x = (place_x == 0) | (place_x == size_x - 1)
    edge_y = (place_y == 0) | (place_y == size_y - 1)
    slot_x = jnp.where(edge_x, place_r % 2 == 1, ~upper_x)
    slot_y = ~upper_y
    lane = lax.broadcasted_iota(jnp.int32, (1, skel), 1)
    own_half = (lane // half) == place_y % 2
    own_quarter = (lane // quarter) == 2 * (place_x % 2) + place_y % 2

    def relative(blocks):
        cube = blocks.reshape((3, 3) + blocks.shape[1:])
        cube = jnp.where(upper_x, cube, cube[::-1])
        return jnp.where(upper_y, cube, cube[:, ::-1])

    def member(order):
        return (order[:, None] == lax.broadcasted_iota(jnp.int32, (1, order.shape[0]), 1)).astype(jnp.float32)

    def pick(values, chosen):
        return dot_t(values, chosen)

    def both(values, axis_groups):
        return lax.all_gather(values, AXES, axis_index_groups=axis_groups)

    def other_of(pair):
        return jnp.where(upper_x, pair[0], pair[1])

    def outside(along, across):
        toward = jnp.stack([along, across])
        first = jnp.where(slot_y, toward[1], toward[0])
        second = jnp.where(slot_y, toward[0], toward[1])
        got = lax.all_to_all(
            jnp.stack([first, second, first, second]), AXES, 0, 0, axis_index_groups=groups.shifted
        )
        beside = jnp.where(slot_x, got[:2], got[2:])
        mine = jnp.where(slot_x, got[2:], got[:2])
        out_x = jnp.where(slot_y, beside[1], beside[0])
        out_xy = jnp.where(slot_y, beside[0], beside[1])
        out_y = jnp.where(slot_y, mine[0], mine[1])
        return (
            jnp.where(edge_x, 0.0, out_x),
            jnp.where(edge_y, 0.0, out_y),
            jnp.where(edge_x | edge_y, 0.0, out_xy),
        )

    near = near_one[0, 0].astype(jnp.float32)[:, None, None]
    blocks_one = relative(near * couple_one[0, 0])
    blocks_two = relative(couple_two[0, 0])
    blocks_three = relative(couple_three[0, 0])
    lift_one = relative(near * spread_one[0, 0])
    lift_two = relative(spread_two[0, 0])
    lift_three = relative(spread_three[0, 0])

    def third(corner, edge):
        return lanes(blocks_three[corner], blocks_three[edge], lift_three[corner], lift_three[edge])

    inverses = lanes(solve_two[0, 0], solve_three[0, 0], top_three[0, 0])
    to_row = [
        blocks_one[1, 0],
        blocks_one[2, 0],
        blocks_one[0, 0],
        inverses,
        jnp.where(same, third((2, 0), (1, 0)), third((2, 0), (2, 1))),
        jnp.where(same, third((0, 0), (0, 1)), third((0, 0), (1, 0))),
    ] + [lanes(blocks_two[side, 0], lift_two[side, 0]) for side in range(3)]
    swap = [(i, i ^ 1) for i in range(size_y)]
    row = lax.ppermute(jnp.stack(to_row), "by", swap)

    chosen_one = member(order_one[0, 0])
    candidates = dot_t(rhs_nodes[0, 0], leaf_map[0, 0])
    picked_one = pick(candidates, chosen_one)
    redund_one = picked_one[:, skel:]
    zone_one = dot(redund_one, solve_one[0, 0])
    base_one = picked_one[:, :skel] - dot(redund_one, interp_one[0, 0])
    field = dot(forward[0, 0], derivative[0, 0])

    out_x, out_y, out_xy = outside(zone_one, zone_one)

    to_side = jnp.stack(
        [
            blocks_one[0, 1],
            blocks_one[0, 2],
            row[2],
            inverses,
            row[3],
            jnp.where(same, third((0, 2), (1, 2)), third((0, 2), (0, 1))),
            row[5],
        ]
    )
    orders = order_two[0, 0].astype(jnp.float32).reshape(1, 2, skel)
    orders = jnp.pad(orders, ((0, 0), (0, skel - 2), (0, 0)))
    side = other_of(both(rows(to_side, orders), groups.sibling))

    part_own = base_one - dot(
        lanes(zone_one, out_x, out_y, out_xy),
        rows(blocks_one[1, 1], blocks_one[2, 1], blocks_one[1, 2], blocks_one[2, 2]),
    )
    part_side = -dot(lanes(zone_one, out_y), rows(side[0], side[1]))
    part_row = -dot(lanes(zone_one, out_x), rows(row[0], row[1]))
    part_diag = -dot(zone_one, side[2])
    parts = jnp.stack([part_own, part_side, part_row, part_diag])
    parts = parts + other_of(both(parts, groups.diagonal))[::-1]
    parts = parts + other_of(both(parts, groups.sibling))[jnp.array([1, 0, 3, 2])]

    def by_row(first, second):
        return jnp.where(upper_y, lanes(second, first), lanes(first, second))

    def by_side(first, second):
        return jnp.where(upper_x, lanes(second, first), lanes(first, second))

    chosen_two = member(order_two[0, 0])
    chosen_side = member(side[7, :2].reshape(-1).astype(jnp.int32))
    solve_own = by_row(solve_two[0, 0], row[3][:, :half])
    solve_side = by_row(side[3][:, :half], side[4][:, :half])
    picked_two = pick(by_row(parts[0], parts[2]), chosen_two)
    redund_two = picked_two[:, skel:]
    zone_two = dot(redund_two, solve_own)
    redund_side = pick(by_row(parts[1], parts[3]), chosen_side[skel:])
    zone_side = dot(redund_side, solve_side)

    def second_level(values_own, values_side, kept, native, far):
        gone_x, gone_y, gone_xy = outside(
            jnp.stack([values_own, values_side]), jnp.stack([values_own, values_side])
        )
        here = dot(lanes(*kept[0], values_side, values_own, gone_x[0]), rows(*kept[1], *native))
        beyond = dot(lanes(gone_y[1], gone_y[0], gone_xy[0]), rows(*far))
        return here, beyond

    def all_parts(part):
        pair = jnp.stack([part, other_of(both(part, groups.diagonal))])
        return pair + other_of(both(pair, groups.sibling))[::-1]

    here, beyond = second_level(
        zone_two,
        zone_side,
        ([redund_two], [interp_two[0, 0]]),
        [blocks_two[a, 1] for a in range(3)],
        [by_row(blocks_two[a, 2], row[6 + a][:, :half]) for a in range(3)],
    )
    part = jnp.where(own_half, picked_two[:, :skel] - lanes(here, here), 0.0) - beyond
    skel_two = all_parts(part)

    def by_box(own, along, across, far):
        return jnp.where(
            upper_x,
            by_row_pairs(along, far, own, across),
            by_row_pairs(own, across, along, far),
        )

    def by_row_pairs(first, second, third_, fourth):
        return lanes(by_row(first, second), by_row(third_, fourth))

    def quarters(place):
        return [where[:, place * quarter : (place + 1) * quarter] for where in (side[5], row[4], side[6])]

    def whole(own, place):
        along, across, far = quarters(place)
        return by_box(own, along, across, far)

    corner_down, corner_up = whole(blocks_three[2, 2], 0), whole(lift_three[2, 2], 2)
    edge_down = whole(jnp.where(same, blocks_three[2, 1], blocks_three[1, 2]), 1)
    edge_up = whole(jnp.where(same, lift_three[2, 1], lift_three[1, 2]), 3)
    solve_whole = by_box(
        *[part_[:, half : half + quarter] for part_ in (inverses, side[3], row[3], side[4])]
    )
    top_whole = by_box(*[part_[:, half + quarter :] for part_ in (inverses, side[3], row[3], side[4])])

    chosen_three = member(order_three[0, 0])
    picked_three = pick(by_side(skel_two[0], skel_two[1]), chosen_three)
    redund_three = picked_three[:, skel:]
    zone_three = dot(redund_three, solve_whole)

    def third_level(values, corner, edge):
        gone_x, gone_y, gone_xy = outside(values, values)
        return dot(lanes(gone_xy, jnp.where(same, gone_x, gone_y)), rows(corner, edge))

    def total(part):
        part = part + other_of(both(part, groups.diagonal))
        return part + other_of(both(part, groups.sibling))

    def tiled(values):
        return lanes(values, values, values, values)

    here = dot(lanes(redund_three, zone_three), rows(interp_three[0, 0], blocks_three[1, 1]))
    part = jnp.where(own_quarter, picked_three[:, :skel] - tiled(here), 0.0)
    skel_three = total(part - third_level(zone_three, corner_down, edge_down))
    value_three = dot(skel_three, top_whole)

    here = dot(value_three, back_three[0, 0] + lift_three[1, 1])
    part = jnp.where(own_quarter, zone_three - tiled(here), 0.0)
    rest_three = total(part - third_level(value_three, corner_up, edge_up))
    final_three = dot(lanes(value_three, rest_three), chosen_three)

    low, high = final_three[:, :skel], final_three[:, skel:]
    value_two = jnp.where(upper_x, high, low)
    value_side = jnp.where(upper_x, low, high)
    here, beyond = second_level(
        value_two,
        value_side,
        ([], []),
        [lift_two[0, 1], lift_two[1, 1] + back_two[0, 0], lift_two[2, 1]],
        [by_row(lift_two[a, 2], row[6 + a][:, half:]) for a in range(3)],
    )
    part = jnp.where(own_half, zone_two - lanes(here, here), 0.0) - beyond
    rest_two = all_parts(part)
    final_two = dot(lanes(value_two, rest_two[0]), chosen_two)
    final_side = dot(lanes(value_side, rest_two[1]), chosen_side)

    def rows_of(final):
        low, high = final[:, :skel], final[:, skel:]
        return jnp.where(upper_y, high, low), jnp.where(upper_y, low, high)

    value_own, value_row = rows_of(final_two)
    value_along, value_diag = rows_of(final_side)
    gone_x, gone_y, gone_xy = outside(
        jnp.stack([value_own, value_row]), jnp.stack([value_own, value_along])
    )
    around = lanes(
        value_diag, value_along, gone_y[1], value_row, value_own, gone_y[0], gone_x[1], gone_x[0], gone_xy[0]
    )
    lifts = [lift_one[a, b] for a in range(3) for b in range(3)]
    lifts[4] = lifts[4] + back_one[0, 0]
    rest_one = zone_one - dot(around, rows(*lifts))
    final_one = dot(lanes(value_own, rest_one), chosen_one)
    adjoint = dot(final_one, leaf_map[0, 0])

    count = lax.axis_size("rhs")
    weight = jnp.sum(adjoint * field, axis=0, keepdims=True) / (count * adjoint.shape[0])
    panel = lax.broadcasted_iota(jnp.int32, (PANELS, 1), 0)
    inside = (node_panel[0] == panel).astype(jnp.float32)
    shares = dot_t(weight, inside).reshape(count, PANELS // count)
    shares = lax.all_to_all(shares, "rhs", 0, 0, tiled=True)
    gradient = jnp.sum(shares, axis=0)
    return adjoint[None, None], gradient[None, None]


def solution(mesh):
    box = P("bx", "by")
    columns = P("bx", "by", "rhs", None)
    groups = Groups(mesh.shape["bx"], mesh.shape["by"], mesh.shape["rhs"])
    return jax.shard_map(
        functools.partial(on_device, groups),
        mesh=mesh,
        in_specs=(columns, columns) + (box,) * 23,
        out_specs=(columns, P("bx", "by", "rhs")),
        check_vma=False,
    )
```

time: 212 us -> 191 us (0.901)
  starting transfers between devices: 120 us -> 44.7 us
  local copies, waits for them, and re-layouts: 11 us -> 41.6 us
  blocking collectives: 8.71 us -> 37.6 us
  waiting for transfers between devices: 50.2 us -> 21.8 us
  between operations: 2.21 us -> 15.2 us
  other arithmetic: 12.3 us -> 20.3 us
    ppermute x37 -> x1, starting transfers between devices: 120 us -> 4.36 us  [on_device(): row = lax.ppermute(jnp.stack(to_row), 'by', swap)]
    ppermute x37 -> x1, waiting for transfers between devices: 50.2 us -> 0.01 us  [on_device(): row = lax.ppermute(jnp.stack(to_row), 'by', swap)]
    all_to_all x0 -> x6, starting transfers between devices: none -> 40.4 us  [outside(): lax.all_to_all(jnp.stack([first, second, first, second]), AXES, 0, 0, axi...]
    all_gather x0 -> x10, blocking collectives: none -> 29.7 us  [both(): return lax.all_gather(values, AXES, axis_index_groups=axis_groups)]
    unnamed x54 -> x217, local copies, waits for them, and re-layouts: 5.67 us -> 31.2 us
    all_to_all x0 -> x6, waiting for transfers between devices: none -> 13.9 us  [outside(): lax.all_to_all(jnp.stack([first, second, first, second]), AXES, 0, 0, axi...]
    sort x3 -> x0, other arithmetic: 10.2 us -> none  [placed_cols(): return jnp.take(values, jnp.argsort(order), axis=1)]
    unnamed x1 -> x0, blocking collectives: 8.71 us -> none
  transfers between devices with their start and end apart: 37 -> 8, of which waited for: 23 -> 6; matrix products, arithmetic and copies ran while one was open for 4% -> 8% of each run, Pallas kernels for 0% -> 0%
where the time goes in v1:
time: 191 us; the launch traced here: 189 us
  starting transfers between devices  44.7 us (23%)
  local copies, waits for them, and re-layouts  41.6 us (22%)
  blocking collectives  37.6 us (20%)
  waiting for transfers between devices  21.8 us (11%)
  other arithmetic  20.3 us (11%)
  between operations  15.2 us (8%)
  matrix products  7.27 us (4%)
    all_to_all x6, starting transfers between devices, outside(): lax.all_to_all(jnp.stack([first, second, first, second]), AXES, 0, 0, axi...  40.4 us
    unnamed x217, local copies, waits for them, and re-layouts  31.2 us
    all_gather x10, blocking collectives, both(): return lax.all_gather(values, AXES, axis_index_groups=axis_groups)  29.7 us
    all_to_all x6, waiting for transfers between devices, outside(): lax.all_to_all(jnp.stack([first, second, first, second]), AXES, 0, 0, axi...  13.9 us
    all_to_all x1, blocking collectives, on_device(): shares = lax.all_to_all(shares, 'rhs', 0, 0, tiled=True)  7.91 us
    all_gather x1, waiting for transfers between devices, both(): return lax.all_gather(values, AXES, axis_index_groups=axis_groups)  7.87 us
    dot_general x25, matrix products, dot(): lax.dot_general(left, right, (((1,), (0,)), ((), ())), precision=PRECISIO...  5.97 us
    ppermute x1, starting transfers between devices, on_device(): row = lax.ppermute(jnp.stack(to_row), 'by', swap)  4.36 us
  transfers between devices with their start and end apart: 8, of which 6 were waited for; matrix products, arithmetic and copies ran while one was open for 8% of the time, Pallas kernels for 0%

profile of v1, /device:TPU:1, one launch (start us, length us, event | category | flops | bytes accessed | tf_op | source)
XLA Modules:
  0.0 188.6 jit_solution(3896010406506061500)
XLA Ops:
  7.2 1.2 copy.48
  9.5 0.7 copy.52
  10.3 1.0 broadcast_multiply_fusion
  15.1 0.8 slice_bitcast_fusion.13
  15.8 0.8 slice_bitcast_fusion.18
  16.6 0.8 slice_bitcast_fusion.27
  17.5 0.8 slice_bitcast_fusion.12
  19.3 0.7 constant_dynamic-update-slice_fusion.5
  20.0 0.8 constant_dynamic-update-slice_fusion.4
  20.8 0.8 constant_dynamic-update-slice_fusion.3
  21.6 0.7 constant_dynamic-update-slice_fusion.2
  22.3 0.7 constant_dynamic-update-slice_fusion.1
  23.0 0.7 constant_dynamic-update-slice_fusion
  23.7 4.4 %collective-permute-start = (f32[9,128,128]{2,1,0:T(8,128)}, f32[9,128,128]{2,1,0:T(8,128)S(1)}, u32[]{:S(2)}, u32[]{:S(2)}) collective-permute-start(f32[9,128,128]{2,1,0:T(8,128)} %constant_dynamic-update-slice_fusion), channel_id=1, source_target_pairs={{0,4},{4,0},{8,12},{12,8},{16,20},{20,16},{24,28},{28,24},{32,36},... | collective-permute-start | bytes 1769480 | tf_op jit(solution)/shard_map/ppermute | solution.py:154
  30.4 12.1 %all-to-all-start = ((f32[4,16,128]{2,1,0:T(8,128)}), f32[4,16,128]{2,1,0:T(8,128)}, u32[]{:S(2)}, u32[]{:S(2)}) async-start(f32[4,16,128]{2,1,0:T(8,128)} %stack.62), calls=%async_computation | async-start | bytes 65536 | tf_op jit(solution)/shard_map/all_to_all | solution.py:119
  42.6 0.7 slice_bitcast_fusion.60
  46.2 0.7 copy.49
  47.7 0.7 copy.51
  48.6 0.8 copy-done.43
  50.0 0.8 slice_select_fusion.18
  51.4 1.7 fusion.4
  55.0 0.8 fusion.249
  56.4 0.8 copy-done.4
  57.6 0.7 copy-done.17
  58.3 0.7 maximum_select_fusion.32
  59.2 0.7 copy-done.13
  60.1 0.7 copy-done.20
  61.9 0.7 copy-done.12
  62.7 0.7 copy-done.16
  63.5 0.7 maximum_select_fusion.9
  64.3 0.8 copy-done.11
  65.0 0.7 maximum_select_fusion.8
  65.8 0.8 copy-done.10
  66.6 0.7 maximum_select_fusion.7
  67.3 7.9 %all-gather.13.cloned.1.call-done = f32[16,128,128]{2,1,0:T(8,128)} async-done(((f32[8,128,128]{2,1,0:T(8,128)}), f32[16,128,128]{2,1,0:T(8,128)}) %all-gather.13.cloned.1.call-update) | async-done | bytes 1048592 | tf_op jit(solution)/shard_map/all_gather | solution.py:110
  75.2 1.3 fusion.262
  76.6 0.8 fusion.248
  77.4 0.8 fusion.247
  78.5 0.7 iota_compare_fusion.3
  79.9 4.0 %all-gather.1 = f32[8,16,128]{2,1,0:T(8,128)S(1)} all-gather(f32[4,16,128]{2,1,0:T(8,128)S(1)} %pad_maximum_fusion.1), channel_id=3, replica_groups={{0,68},{1,69},{2,70},{3,71},{4,64},{5,65},{6,66},{7,67},{8,76},{9,77},{..., dimensions={0}, use_global_device_ids=true | all-gather | bytes 98304 | tf_op jit(solution)/shard_map/all_gather | solution.py:110
  83.9 1.9 all-gather.2
  85.8 0.8 gather_fusion
  90.1 6.1 %all-to-all-start.1 = ((f32[4,2,16,128]{3,2,1,0:T(8,128)}), f32[4,2,16,128]{3,2,1,0:T(8,128)S(1)}, u32[]{:S(2)}, u32[]{:S(2)}) async-start(f32[4,2,16,128]{3,2,1,0:T(8,128)} %stack.144), calls=%async_computation.1 | async-start | bytes 131072 | tf_op jit(solution)/shard_map/all_to_all | solution.py:119
  96.5 0.7 copy-done.28
  98.2 1.7 all-to-all-done.1
  101.8 3.8 %all-gather.3 = f32[32,128]{1,0:T(8,128)S(1)} all-gather(f32[16,128]{1,0:T(8,128)S(1)} %convolution_subtract_fusion.4), channel_id=5, replica_groups={{0,68},{1,69},{2,70},{3,71},{4,64},{5,65},{6,66},{7,67},{8,76},{9,77},{..., dimensions={0}, use_global_device_ids=true | all-gather | bytes 24576 | tf_op jit(solution)/shard_map/all_gather | solution.py:110
  105.7 1.9 %all-gather.4 = f32[4,16,128]{2,1,0:T(8,128)S(1)} all-gather(f32[2,16,128]{2,1,0:T(8,128)S(1)} %pad_maximum_fusion.9), channel_id=6, replica_groups={{0,64},{1,65},{2,66},{3,67},{4,68},{5,69},{6,70},{7,71},{8,72},{9,73},{..., dimensions={0}, use_global_device_ids=true | all-gather | bytes 49152 | tf_op jit(solution)/shard_map/all_gather | solution.py:110
  109.8 5.6 %all-to-all-start.2 = ((f32[4,16,128]{2,1,0:T(8,128)}), f32[4,16,128]{2,1,0:T(8,128)S(1)}, u32[]{:S(2)}, u32[]{:S(2)}) async-start(f32[4,16,128]{2,1,0:T(8,128)} %stack.147), calls=%async_computation.2 | async-start | bytes 65536 | tf_op jit(solution)/shard_map/all_to_all | solution.py:119
  115.5 3.2 %all-to-all-done.2 = f32[4,16,128]{2,1,0:T(8,128)S(1)} async-done(((f32[4,16,128]{2,1,0:T(8,128)}), f32[4,16,128]{2,1,0:T(8,128)S(1)}, u32[]{:S(2)}, u32[]{:S(2)}) %all-to-all-start.2) | async-done | bytes 32800 | tf_op jit(solution)/shard_map/all_to_all | solution.py:119
  119.6 4.1 %all-gather.5 = f32[32,128]{1,0:T(8,128)S(1)} all-gather(f32[16,128]{1,0:T(8,128)S(1)} %convolution_subtract_fusion.3), channel_id=7, replica_groups={{0,68},{1,69},{2,70},{3,71},{4,64},{5,65},{6,66},{7,67},{8,76},{9,77},{..., dimensions={0}, use_global_device_ids=true | all-gather | bytes 24576 | tf_op jit(solution)/shard_map/all_gather | solution.py:110
  123.7 1.9 %all-gather.6 = f32[32,128]{1,0:T(8,128)S(1)} all-gather(f32[16,128]{1,0:T(8,128)S(1)} %fusion.194), channel_id=8, replica_groups={{0,64},{1,65},{2,66},{3,67},{4,68},{5,69},{6,70},{7,71},{8,72},{9,73},{..., dimensions={0}, use_global_device_ids=true | all-gather | bytes 24576 | tf_op jit(solution)/shard_map/all_gather | solution.py:110
  126.5 5.5 %all-to-all-start.3 = ((f32[4,16,128]{2,1,0:T(8,128)}), f32[4,16,128]{2,1,0:T(8,128)S(1)}, u32[]{:S(2)}, u32[]{:S(2)}) async-start(f32[4,16,128]{2,1,0:T(8,128)} %stack.148), calls=%async_computation.3 | async-start | bytes 65536 | tf_op jit(solution)/shard_map/all_to_all | solution.py:119
  132.0 3.2 %all-to-all-done.3 = f32[4,16,128]{2,1,0:T(8,128)S(1)} async-done(((f32[4,16,128]{2,1,0:T(8,128)}), f32[4,16,128]{2,1,0:T(8,128)S(1)}, u32[]{:S(2)}, u32[]{:S(2)}) %all-to-all-start.3) | async-done | bytes 32800 | tf_op jit(solution)/shard_map/all_to_all | solution.py:119
  135.4 4.1 %all-gather.7 = f32[32,128]{1,0:T(8,128)S(1)} all-gather(f32[16,128]{1,0:T(8,128)S(1)} %convolution_subtract_fusion.2), channel_id=9, replica_groups={{0,68},{1,69},{2,70},{3,71},{4,64},{5,65},{6,66},{7,67},{8,76},{9,77},{..., dimensions={0}, use_global_device_ids=true | all-gather | bytes 24576 | tf_op jit(solution)/shard_map/all_gather | solution.py:110
  139.5 1.9 %all-gather.8 = f32[32,128]{1,0:T(8,128)S(1)} all-gather(f32[16,128]{1,0:T(8,128)S(1)} %fusion.187), channel_id=10, replica_groups={{0,64},{1,65},{2,66},{3,67},{4,68},{5,69},{6,70},{7,71},{8,72},{9,73},{..., dimensions={0}, use_global_device_ids=true | all-gather | bytes 24576 | tf_op jit(solution)/shard_map/all_gather | solution.py:110
  142.3 5.6 %all-to-all-start.4 = ((f32[4,2,16,128]{3,2,1,0:T(8,128)}), f32[4,2,16,128]{3,2,1,0:T(8,128)S(1)}, u32[]{:S(2)}, u32[]{:S(2)}) async-start(f32[4,2,16,128]{3,2,1,0:T(8,128)} %stack.152), calls=%async_computation.4 | async-start | bytes 131072 | tf_op jit(solution)/shard_map/all_to_all | solution.py:119
  148.0 0.7 copy-done.8
  148.9 2.4 %all-to-all-done.4 = f32[4,2,16,128]{3,2,1,0:T(8,128)S(1)} async-done(((f32[4,2,16,128]{3,2,1,0:T(8,128)}), f32[4,2,16,128]{3,2,1,0:T(8,128)S(1)}, u32[]{:S(2)}, u32[]{:S(2)}) %all-to-all-start.4) | async-done | bytes 65568 | tf_op jit(solution)/shard_map/all_to_all | solution.py:119
  151.4 0.8 copy-done.46
  153.3 3.8 %all-gather.9 = f32[32,128]{1,0:T(8,128)S(1)} all-gather(f32[16,128]{1,0:T(8,128)S(1)} %convolution_subtract_fusion.1), channel_id=11, replica_groups={{0,68},{1,69},{2,70},{3,71},{4,64},{5,65},{6,66},{7,67},{8,76},{9,77},{..., dimensions={0}, use_global_device_ids=true | all-gather | bytes 24576 | tf_op jit(solution)/shard_map/all_gather | solution.py:110
  157.1 2.3 %all-gather.10 = f32[4,16,128]{2,1,0:T(8,128)S(1)} all-gather(f32[2,16,128]{2,1,0:T(8,128)S(1)} %pad_maximum_fusion.11), channel_id=12, replica_groups={{0,64},{1,65},{2,66},{3,67},{4,68},{5,69},{6,70},{7,71},{8,72},{9,73},{..., dimensions={0}, use_global_device_ids=true | all-gather | bytes 49152 | tf_op jit(solution)/shard_map/all_gather | solution.py:110
  161.1 5.5 %all-to-all-start.5 = ((f32[4,2,16,128]{3,2,1,0:T(8,128)}), f32[4,2,16,128]{3,2,1,0:T(8,128)S(1)}, u32[]{:S(2)}, u32[]{:S(2)}) async-start(f32[4,2,16,128]{3,2,1,0:T(8,128)} %pad_maximum_fusion), calls=%async_computation.5 | async-start | bytes 131072 | tf_op jit(solution)/shard_map/all_to_all | solution.py:119
  166.6 3.4 %all-to-all-done.5 = f32[4,2,16,128]{3,2,1,0:T(8,128)S(1)} async-done(((f32[4,2,16,128]{3,2,1,0:T(8,128)}), f32[4,2,16,128]{3,2,1,0:T(8,128)S(1)}, u32[]{:S(2)}, u32[]{:S(2)}) %all-to-all-start.5) | async-done | bytes 65568 | tf_op jit(solution)/shard_map/all_to_all | solution.py:119
  173.3 7.9 %all_to_all.39 = f32[4,1,4]{2,1,0:T(1,128)S(1)} all-to-all(f32[4,1,4]{2,1,0:T(1,128)S(1)} %convolution_bitcast_fusion), channel_id=1, replica_groups=mesh['bx'=8,'by'=16,'rhs'=4] {'rhs'}, dimensions={0} | all-to-all | bytes 128 | tf_op jit(solution)/shard_map/all_to_all | solution.py:319
  (345 shorter events, 37.2 us)
Async XLA Ops:
  7.2 20.9 %copy-start = (f32[1,1,256,256]{3,2,1,0:T(8,128)S(1)}, f32[1,1,256,256]{3,2,1,0:T(8,128)}, u32[]{:S(2)}) copy-start(f32[1,1,256,256]{3,2,1,0:T(8,128)} %param.28) | copy-start | bytes 786436
  7.2 1.3 copy-start.7
  8.9 1.4 copy-start.5
  8.9 1.4 copy-start.6
  12.1 0.9 copy-start.65
  12.8 0.9 copy-start.35
  13.7 0.9 copy-start.36
  16.6 0.8 copy-start.19
  17.5 1.2 copy-start.3
  23.0 5.1 %copy-start.73 = (f32[1,1,16,256]{3,2,1,0:T(8,128)S(1)}, f32[1,1,16,256]{3,2,1,0:T(8,128)}, u32[]{:S(2)}) copy-start(f32[1,1,16,256]{3,2,1,0:T(8,128)} %param.26) | copy-start | bytes 49156
  23.7 29.3 %collective-permute-start = (f32[9,128,128]{2,1,0:T(8,128)}, f32[9,128,128]{2,1,0:T(8,128)S(1)}, u32[]{:S(2)}, u32[]{:S(2)}) collective-permute-start(f32[9,128,128]{2,1,0:T(8,128)} %constant_dynamic-update-slice_fusion), channel_id=1, source_target_pairs={{0,4},{4,0},{8,12},{12,8},{16,20},{20,16},{24,28},{28,24},{32,36},... | collective-permute-start | bytes 1769480 | tf_op jit(solution)/shard_map/ppermute | solution.py:154
  28.3 0.9 copy-start.56
  28.8 19.6 %copy-start.2 = (f32[3,3,128,128]{3,2,1,0:T(8,128)S(1)}, f32[3,3,128,128]{3,2,1,0:T(8,128)}, u32[]{:S(2)}) copy-start(f32[3,3,128,128]{3,2,1,0:T(8,128)} %get-tuple-element.134) | copy-start | bytes 1769476
  30.4 19.6 %all-to-all-start = ((f32[4,16,128]{2,1,0:T(8,128)}), f32[4,16,128]{2,1,0:T(8,128)}, u32[]{:S(2)}, u32[]{:S(2)}) async-start(f32[4,16,128]{2,1,0:T(8,128)} %stack.62), calls=%async_computation | async-start | bytes 65536 | tf_op jit(solution)/shard_map/all_to_all | solution.py:119
  42.6 32.6 %all-gather.13.cloned.1.call-start = ((), (), s32[]{:S(2)}) async-start(), calls=%async_computation.7 | async-start | bytes 1572864 | tf_op jit(solution)/shard_map/all_gather | solution.py:110
  42.6 1.8 copy-start.86
  42.6 2.4 %copy-start.57 = (f32[1,1,128,128]{3,2,1,0:T(8,128)S(1)}, f32[1,1,128,128]{3,2,1,0:T(8,128)}, u32[]{:S(2)}) copy-start(f32[1,1,128,128]{3,2,1,0:T(8,128)} %param.33) | copy-start | bytes 196612
  43.3 1.7 copy-start.78
  45.0 1.2 copy-start.66
  45.6 1.3 copy-start.18
  48.5 0.8 copy-start.43
  50.0 1.4 copy-start.60
  50.0 1.4 copy-start.61
  50.8 2.2 %copy-start.69 = (f32[16,128]{1,0:T(8,128)}, f32[16,128]{1,0:T(8,128)S(1)}, u32[]{:S(2)}) copy-start(f32[16,128]{1,0:T(8,128)S(1)} %get-tuple-element.133) | copy-start | bytes 24580
  53.1 0.8 copy-start.26
  53.1 0.9 copy-start.27
  53.2 0.9 copy-start.24
  53.2 0.9 copy-start.25
  57.4 0.8 copy-start.17
  59.1 0.9 copy-start.34
  60.0 0.9 copy-start.21
  60.0 0.9 copy-start.70
  60.9 0.9 copy-start.33
  61.7 0.9 copy-start.32
  76.5 1.9 %copy-start.1 = (f32[16,128,128]{2,1,0:T(8,128)S(1)}, f32[16,128,128]{2,1,0:T(8,128)}, u32[]{:S(2)}) copy-start(f32[16,128,128]{2,1,0:T(8,128)} %all-gather.13.cloned.1.call-done) | copy-start | bytes 3145732
  76.6 7.3 %copy-start.37 = (f32[1,16,128]{2,1,0:T(8,128)}, f32[1,16,128]{2,1,0:T(8,128)S(1)}, u32[]{:S(2)}) copy-start(f32[1,16,128]{2,1,0:T(8,128)S(1)} %fusion.1) | copy-start | bytes 24580
  79.9 4.0 %copy-start.39 = (f32[1,16,128]{2,1,0:T(8,128)}, f32[1,16,128]{2,1,0:T(8,128)S(1)}, u32[]{:S(2)}) copy-start(f32[1,16,128]{2,1,0:T(8,128)S(1)} %fusion.3) | copy-start | bytes 24580
  85.8 0.8 copy-start.40
  85.8 0.8 copy-start.42
  90.1 6.2 %copy-start.29 = (f32[128,32]{1,0:T(8,128)S(1)}, f32[128,32]{1,0:T(8,128)}, u32[]{:S(2)}) copy-start(f32[128,32]{1,0:T(8,128)} %get-tuple-element.84) | copy-start | bytes 49156
  90.1 6.2 %copy-start.31 = (f32[128,32]{1,0:T(8,128)S(1)}, f32[128,32]{1,0:T(8,128)}, u32[]{:S(2)}) copy-start(f32[128,32]{1,0:T(8,128)} %get-tuple-element.80) | copy-start | bytes 49156
  90.1 9.7 %all-to-all-start.1 = ((f32[4,2,16,128]{3,2,1,0:T(8,128)}), f32[4,2,16,128]{3,2,1,0:T(8,128)S(1)}, u32[]{:S(2)}, u32[]{:S(2)}) async-start(f32[4,2,16,128]{3,2,1,0:T(8,128)} %stack.144), calls=%async_computation.1 | async-start | bytes 131072 | tf_op jit(solution)/shard_map/all_to_all | solution.py:119
  96.4 0.8 copy-start.28
  96.4 0.9 copy-start.30
  98.0 1.9 %copy-start.49 = (f32[128,64]{1,0:T(8,128)S(1)}, f32[128,64]{1,0:T(8,128)}, u32[]{:S(2)}) copy-start(f32[128,64]{1,0:T(8,128)} %get-tuple-element.26) | copy-start | bytes 98308
  98.0 1.9 %copy-start.58 = (f32[1,1,128,64]{3,2,1,0:T(8,128)S(1)}, f32[1,1,128,64]{3,2,1,0:T(8,128)}, u32[]{:S(2)}) copy-start(f32[1,1,128,64]{3,2,1,0:T(8,128)} %copy.49) | copy-start | bytes 98308
  99.9 0.8 copy-start.48
  99.9 0.9 copy-start.47
  100.8 0.9 copy-start.52
  100.8 0.9 copy-start.53
  100.8 0.9 copy-start.80
  109.8 5.6 %copy-start.54 = (f32[128,32]{0,1:T(8,128)S(1)}, f32[128,32]{0,1:T(8,128)}, u32[]{:S(2)}) copy-start(f32[128,32]{0,1:T(8,128)} %copy.50) | copy-start | bytes 49156
  109.8 5.6 %slice-start = ((f32[16,256]{1,0:T(8,128)}), f32[16,128]{1,0:T(8,128)S(1)}, s32[]{:S(2)}) async-start(f32[16,256]{1,0:T(8,128)} %copy-done.62), calls=%async_computation.8 | async-start | bytes 16384 | tf_op jit(solution)/shard_map/slice | solution.py:257
  109.8 5.6 %copy-start.75 = (f32[1,1,128,32]{2,3,1,0:T(8,128)S(1)}, f32[1,1,128,32]{2,3,1,0:T(8,128)}, u32[]{:S(2)}) copy-start(f32[1,1,128,32]{2,3,1,0:T(8,128)} %param.45) | copy-start | bytes 49156
  109.8 8.9 %all-to-all-start.2 = ((f32[4,16,128]{2,1,0:T(8,128)}), f32[4,16,128]{2,1,0:T(8,128)S(1)}, u32[]{:S(2)}, u32[]{:S(2)}) async-start(f32[4,16,128]{2,1,0:T(8,128)} %stack.147), calls=%async_computation.2 | async-start | bytes 65536 | tf_op jit(solution)/shard_map/all_to_all | solution.py:119
  125.8 6.1 %copy-start.23 = (f32[1,1,128,32]{3,2,1,0:T(8,128)S(1)}, f32[1,1,128,32]{3,2,1,0:T(8,128)}, u32[]{:S(2)}) copy-start(f32[1,1,128,32]{3,2,1,0:T(8,128)} %copy.51) | copy-start | bytes 49156
  126.5 8.8 %all-to-all-start.3 = ((f32[4,16,128]{2,1,0:T(8,128)}), f32[4,16,128]{2,1,0:T(8,128)S(1)}, u32[]{:S(2)}, u32[]{:S(2)}) async-start(f32[4,16,128]{2,1,0:T(8,128)} %stack.148), calls=%async_computation.3 | async-start | bytes 65536 | tf_op jit(solution)/shard_map/all_to_all | solution.py:119
  142.3 5.6 %copy-start.9 = (f32[128,64]{1,0:T(8,128)S(1)}, f32[128,64]{1,0:T(8,128)}, u32[]{:S(2)}) copy-start(f32[128,64]{1,0:T(8,128)} %get-tuple-element.4) | copy-start | bytes 98308
  142.3 9.0 %all-to-all-start.4 = ((f32[4,2,16,128]{3,2,1,0:T(8,128)}), f32[4,2,16,128]{3,2,1,0:T(8,128)S(1)}, u32[]{:S(2)}, u32[]{:S(2)}) async-start(f32[4,2,16,128]{3,2,1,0:T(8,128)} %stack.152), calls=%async_computation.4 | async-start | bytes 131072 | tf_op jit(solution)/shard_map/all_to_all | solution.py:119
  151.3 0.8 copy-start.46
  151.3 0.9 copy-start.45
  151.4 0.9 copy-start.44
  161.1 8.9 %all-to-all-start.5 = ((f32[4,2,16,128]{3,2,1,0:T(8,128)}), f32[4,2,16,128]{3,2,1,0:T(8,128)S(1)}, u32[]{:S(2)}, u32[]{:S(2)}) async-start(f32[4,2,16,128]{3,2,1,0:T(8,128)} %pad_maximum_fusion), calls=%async_computation.5 | async-start | bytes 131072 | tf_op jit(solution)/shard_map/all_to_all | solution.py:119
  170.8 0.9 copy-start.22
  (41 other events, 30.4 us)
Sparse Core Ops, SparseCore 0:
  57.4 17.7 all-gather.12

commit v2 on v0

v2 whole, which is shorter than its diff:
```python
import functools

import jax
import jax.numpy as jnp
from jax import lax
from jax.experimental import pallas as pl
from jax.experimental.pallas import tpu as pltpu
from jax.sharding import PartitionSpec as P

PANELS = 16
SKEL = 128
HALF = SKEL // 2
QUARTER = SKEL // 4
BOX = 2 * SKEL
COLS = 16
VMEM_LIMIT = 8 << 20
AXES = ("bx", "by", "rhs")
VALUES = (COLS, SKEL)
BLOCK = (SKEL, SKEL)


def halves(values):
    high = values.astype(jnp.bfloat16)
    low = (values - high.astype(jnp.float32)).astype(jnp.bfloat16)
    return high, low


def dims(left, rights, contract):
    left = jnp.concatenate(halves(left), axis=0)
    size = left.shape[0] // 2
    result = None
    for right in rights:
        product = lax.dot_general(
            left, right, (((1,), (contract,)), ((), ())), preferred_element_type=jnp.float32
        )
        product = product[:size] + product[size:]
        result = product if result is None else result + product
    return result


def dot(left, right):
    return dims(left, halves(right), 0)


def dot_t(left, right):
    return dims(left, halves(right), 1)


def pick(values, order):
    return dims(values, (chosen(order),), 0)


def place(values, order):
    return dims(values, (chosen(order),), 1)


def lanes(*parts):
    return jnp.concatenate(parts, axis=1)


def stacked(*parts):
    return jnp.concatenate(parts, axis=0)


class Groups:
    def __init__(self, size_x, size_y, size_r):
        def place(i, j, r):
            return (i * size_y + j) * size_r + r

        every = [(i, j, r) for i in range(size_x) for j in range(size_y) for r in range(size_r)]
        self.sibling = [[place(i, j, r), place(i + 1, j, r)] for i, j, r in every if i % 2 == 0]
        self.diagonal = [[place(i, j, r), place(i + 1, j ^ 1, r)] for i, j, r in every if i % 2 == 0]
        self.shifted = []
        self.crossed = []
        for j in range(1, size_y, 2):
            after = (j + 1) % size_y
            for r in range(size_r):
                for i in range(1, size_x - 1, 2):
                    self.shifted.append(
                        [place(i, j, r), place(i, after, r), place(i + 1, j, r), place(i + 1, after, r)]
                    )
                    self.crossed.append(
                        [place(i, j, r), place(i - 1, after, r), place(i + 1, j, r), place(i + 2, after, r)]
                    )
                if r % 2 == 0:
                    for i in (0, size_x - 1):
                        self.shifted.append(
                            [place(i, j, r), place(i, after, r), place(i, j, r + 1), place(i, after, r + 1)]
                        )
                        self.crossed.append(
                            [
                                place(i, j, r),
                                place(i ^ 1, after, r),
                                place(i, j, r + 1),
                                place(i ^ 1, after, r + 1),
                            ]
                        )


class Here:
    def __init__(self, crossed=False):
        x, y, r = (lax.axis_index(axis) for axis in AXES)
        self.c, self.h = lax.rem(x, 2), lax.rem(y, 2)
        side = jnp.where(self.h == 0, 1 - self.c, self.c) if crossed else self.c
        chip = x - self.c
        self.edge_x = ((chip == 0) & (side == 0)) | ((chip == lax.axis_size("bx") - 2) & (side == 1))
        self.edge_y = (y == 0) | (y == lax.axis_size("by") - 1)
        slot_x = jnp.where(self.edge_x, lax.rem(r, 2), 1 - side)
        slot_y = 1 - self.h
        self.slot_y = slot_y
        self.along = 2 * (1 - slot_x) + slot_y
        self.across = 2 * slot_x + 1 - slot_y
        self.corner = 2 * (1 - slot_x) + 1 - slot_y
        side_x = (2 - 2 * side, 1, 2 * side)
        side_y = (2 - 2 * self.h, 1, 2 * self.h)
        self.block = [[3 * a + b for b in side_y] for a in side_x]
        self.same = side == self.h

    def outside(self, got, item=()):
        x = jnp.where(self.edge_x, 0.0, got[(self.along, *item)])
        y = jnp.where(self.edge_y, 0.0, got[(self.across, *item)])
        xy = jnp.where(self.edge_x | self.edge_y, 0.0, got[(self.corner, *item)])
        return x, y, xy

    def by_row(self, own, other):
        return lanes(jnp.where(self.h == 0, own, other), jnp.where(self.h == 0, other, own))

    def own_half(self):
        lane = lax.broadcasted_iota(jnp.int32, VALUES, 1)
        return lane // HALF == self.h

    def own_quarter(self):
        lane = lax.broadcasted_iota(jnp.int32, VALUES, 1)
        return lane // QUARTER == 2 * self.c + self.h


def chosen(order):
    found = lax.broadcasted_iota(jnp.int32, (BOX, BOX), 0) == order
    return jnp.where(found, 1.0, 0.0).astype(jnp.bfloat16)


def four(values):
    return stacked(values, values, values, values)


NAMES = (
    "rhs_nodes",
    "leaf_map",
    "order_one",
    "solve_one",
    "interp_one",
    "near_one",
    "couple_one",
    "spread_one",
    "couple_two",
    "spread_two",
    "couple_three",
    "spread_three",
    "solve_two",
    "solve_three",
    "top_three",
    "interp_two",
    "interp_three",
    "back_one",
    "back_two",
    "back_three",
    "order_two",
    "order_three",
    "node_panel",
    "forward",
    "derivative",
)
GIVEN = (
    "rhs_nodes",
    "forward",
    "leaf_map",
    "derivative",
    "node_panel",
    "order_one",
    "near_one",
    "interp_one",
    "solve_one",
    "couple_one",
    "back_one",
    "spread_one",
    "order_two",
    "interp_two",
    "solve_two",
    "couple_two",
    "back_two",
    "spread_two",
    "order_three",
    "interp_three",
    "solve_three",
    "couple_three",
    "back_three",
    "spread_three",
    "top_three",
)

LIFT_ONE = 0
LEAF = LIFT_ONE + 9 * SKEL
COUPLE_TWO = LEAF + 2 * BOX
SPREAD_TWO = COUPLE_TWO + 6 * HALF
INTERP_TWO = SPREAD_TWO + 6 * HALF
SOLVE_TWO = INTERP_TWO + HALF
COUPLE_THREE = SOLVE_TWO + HALF
SPREAD_THREE = COUPLE_THREE + 3 * QUARTER
INTERP_THREE = SPREAD_THREE + 3 * QUARTER
SOLVE_THREE = INTERP_THREE + QUARTER
TOP_THREE = SOLVE_THREE + QUARTER
NUMBERS = TOP_THREE + QUARTER
FIELD = NUMBERS + 8
ZONE_ONE = FIELD + 2 * COLS
KEPT = (ZONE_ONE + COLS, SKEL)
ORDER_ONE, ORDER_TWO, ORDER_THREE, PANEL_OF = range(0, 8, 2)

SOLVE_OWN, SOLVE_SIDE, SOLVE_ALL, TOP_ALL, COUPLE_ALL, SPREAD_ALL = 0, 1, 2, 3, 4, 6
COUPLE_FAR, SPREAD_FAR, ORDER_SIDE = 8, 11, 14
WHOLE = (ORDER_SIDE * SKEL + 8, SKEL)
SIDE_BLOCKS = 2 * COLS
SIDE_NUMBERS = SIDE_BLOCKS + 3 * SKEL
SIDE = (SIDE_NUMBERS + 8, SKEL)


def numbers_of(ref, row):
    return lanes(ref[row : row + 1], ref[row + 1 : row + 2]).astype(jnp.int32)


def block_of(ref, number):
    return ref[number * SKEL : (number + 1) * SKEL]


def start_kernel(*refs):
    count = len(NAMES)
    source = dict(zip(NAMES, refs[:count]))
    zone, base, row_out, side_out, couple, kept = refs[count : count + 6]
    held = dict(zip(NAMES, refs[count + 6 : -1]))
    sems = refs[-1]
    here = Here()
    copies = {name: pltpu.make_async_copy(source[name], held[name], sems.at[i]) for i, name in enumerate(NAMES)}
    for name in NAMES:
        copies[name].start()

    def read(name):
        copies[name].wait()
        return held[name][...]

    rhs, leaf = read("rhs_nodes"), read("leaf_map")
    candidates = dot_t(rhs, leaf)
    kept[LEAF : LEAF + BOX] = leaf[:, :SKEL]
    kept[LEAF + BOX : LEAF + 2 * BOX] = leaf[:, SKEL:]
    picked = pick(candidates, read("order_one"))
    redund = picked[:, SKEL:]
    values = dot(redund, read("solve_one"))
    zone[...] = values
    kept[ZONE_ONE:] = values
    base[...] = picked[:, :SKEL] - dot(redund, read("interp_one"))
    spots = lax.broadcasted_iota(jnp.int32, (16, 9), 0) == lax.broadcasted_iota(jnp.int32, (16, 9), 1)
    near = jnp.where(spots, read("near_one").astype(jnp.float32), 0.0)
    near = jnp.broadcast_to(jnp.sum(near, axis=1, keepdims=True), VALUES)
    number = lax.broadcasted_iota(jnp.int32, VALUES, 0)

    def scaled(name, a, b):
        n = here.block[a][b]
        weight = jnp.sum(jnp.where(number == n, near, 0.0), axis=0, keepdims=True)
        return weight * held[name][n]

    for name in NAMES[NAMES.index("couple_one") :]:
        copies[name].wait()
    for out, start in ((row_out.at[0], 0), (side_out, 0)):
        out[start : start + HALF] = held["solve_two"][...]
        out[start + HALF : start + HALF + QUARTER] = held["solve_three"][...]
        out[start + HALF + QUARTER : start + SKEL] = held["top_three"][...]
    cross = Here(crossed=True)

    def third(out, start, corner, edge_same, edge_else):
        corner = cross.block[corner[0]][corner[1]]
        edge = jnp.where(
            cross.same, cross.block[edge_same[0]][edge_same[1]], cross.block[edge_else[0]][edge_else[1]]
        )
        for i, (name, n) in enumerate(
            (("couple_three", corner), ("couple_three", edge), ("spread_three", corner), ("spread_three", edge))
        ):
            out[start + i * QUARTER : start + (i + 1) * QUARTER] = held[name][n]

    third(row_out.at[1], 0, (0, 0), (0, 1), (1, 0))
    third(side_out, SKEL, (0, 2), (1, 2), (0, 1))
    third(side_out, 2 * SKEL, (2, 0), (1, 0), (2, 1))
    for a in range(3):
        n = here.block[a][0]
        row_out[2 + a, :HALF] = held["couple_two"][n]
        row_out[2 + a, HALF:] = held["spread_two"][n]
    for a in range(3):
        for b in range(3):
            at = (3 * a + b) * SKEL
            couple[at : at + SKEL] = scaled("couple_one", a, b)
            at = LIFT_ONE + at
            block = scaled("spread_one", a, b)
            kept[at : at + SKEL] = block + held["back_one"][...] if a == b == 1 else block
        for b in (1, 2):
            n = here.block[a][b]
            at = COUPLE_TWO + (2 * a + b - 1) * HALF
            kept[at : at + HALF] = held["couple_two"][n]
            at = SPREAD_TWO + (2 * a + b - 1) * HALF
            block = held["spread_two"][n]
            kept[at : at + HALF] = block + held["back_two"][...] if a == b == 1 else block
    edge = jnp.where(cross.same, cross.block[2][1], cross.block[1][2])
    for i, n in enumerate((4, cross.block[2][2], edge)):
        at = COUPLE_THREE + i * QUARTER
        kept[at : at + QUARTER] = held["couple_three"][n]
        at = SPREAD_THREE + i * QUARTER
        block = held["spread_three"][n]
        kept[at : at + QUARTER] = block + held["back_three"][...] if i == 0 else block
    for name, at in (
        ("interp_two", INTERP_TWO),
        ("solve_two", SOLVE_TWO),
        ("interp_three", INTERP_THREE),
        ("solve_three", SOLVE_THREE),
        ("top_three", TOP_THREE),
    ):
        kept[at : at + held[name].shape[0]] = held[name][...]
    for name, row in (
        ("order_one", ORDER_ONE),
        ("order_two", ORDER_TWO),
        ("order_three", ORDER_THREE),
        ("node_panel", PANEL_OF),
    ):
        numbers = held[name][...].astype(jnp.float32)
        kept[NUMBERS + row : NUMBERS + row + 1] = numbers[:, :SKEL]
        kept[NUMBERS + row + 1 : NUMBERS + row + 2] = numbers[:, SKEL:]
    side_out[3 * SKEL :] = kept[NUMBERS : NUMBERS + 8]
    field = dot(held["forward"][...], held["derivative"][...])
    kept[FIELD : FIELD + COLS] = field[:, :SKEL]
    kept[FIELD + COLS : FIELD + 2 * COLS] = field[:, SKEL:]


def side_kernel(pair, side, out):
    out[:COLS], out[COLS:SIDE_BLOCKS] = pair[0], pair[1]
    out[SIDE_BLOCKS:] = side[...]


def fill(here, boxes, chunk):
    for slot in range(4):
        chunk[slot, 0] = boxes[0]
        chunk[slot, 1] = jnp.where(here.slot_y == slot % 2, boxes[2], boxes[1])


def around(here, got, boxes):
    out_x, out_y, out_xy = here.outside(got, (0,))
    out_x_row = jnp.where(here.edge_x, 0.0, got[here.along, 1])
    out_y_side = jnp.where(here.edge_y, 0.0, got[here.across, 1])
    return lanes(boxes[3], boxes[1], out_y_side, boxes[2], boxes[0], out_y, out_x_row, out_x, out_xy)


def row_kernel(row, sides, chunk, boxes, out):
    here = Here()
    c, d = here.c, 1 - here.c
    for box, (member, number) in enumerate(((c, c), (d, d), (d, c), (c, d))):
        boxes[box] = sides[member, pl.ds(pl.multiple_of(number * COLS, COLS), COLS)]
    fill(here, boxes, chunk)
    out[0], out[1] = row[0], sides[d, SIDE_BLOCKS : SIDE_BLOCKS + SKEL]
    out[2], out[3] = row[1], sides[d, SIDE_BLOCKS + 2 * SKEL : SIDE_BLOCKS + 3 * SKEL]
    for a in range(3):
        out[4 + a] = row[2 + a]


def first_kernel(got, boxes, base, couple, part):
    part[...] = base[...] - dot(around(Here(), got, boxes), couple[...])


def put_together(here, kept, sides, row, whole):
    d = 1 - here.c
    mine, theirs = here.h * HALF, (1 - here.h) * HALF

    def put(number, offset, size, value):
        whole[pl.ds(pl.multiple_of(number * SKEL + offset, size), size)] = value

    def side(block, start, size):
        at = SIDE_BLOCKS + block * SKEL + start
        return sides[d, at : at + size]

    put(SOLVE_OWN, mine, HALF, kept[SOLVE_TWO : SOLVE_TWO + HALF])
    put(SOLVE_OWN, theirs, HALF, row[0, :HALF])
    put(SOLVE_SIDE, mine, HALF, side(0, 0, HALF))
    put(SOLVE_SIDE, theirs, HALF, row[1, :HALF])
    for a in range(3):
        for number, at, start in ((COUPLE_FAR, COUPLE_TWO, 0), (SPREAD_FAR, SPREAD_TWO, HALF)):
            at = at + (2 * a + 1) * HALF
            put(number + a, mine, HALF, kept[at : at + HALF])
            put(number + a, theirs, HALF, row[4 + a, start : start + HALF])
    own_at = (
        SOLVE_THREE,
        TOP_THREE,
        COUPLE_THREE + QUARTER,
        COUPLE_THREE + 2 * QUARTER,
        SPREAD_THREE + QUARTER,
        SPREAD_THREE + 2 * QUARTER,
    )
    for i in range(6):
        start = HALF + i * QUARTER if i < 2 else (i - 2) * QUARTER
        inverse = i < 2
        for c, h, value in (
            (here.c, here.h, kept[own_at[i] : own_at[i] + QUARTER]),
            (d, here.h, side(0 if inverse else 1, start, QUARTER)),
            (here.c, 1 - here.h, row[0 if inverse else 2, start : start + QUARTER]),
            (d, 1 - here.h, row[1 if inverse else 3, start : start + QUARTER]),
        ):
            put(SOLVE_ALL + i, (2 * c + h) * QUARTER, QUARTER, value)
    whole[ORDER_SIDE * SKEL :] = sides[d, SIDE_NUMBERS:]


def second_kernel(sums, kept, sides, row, chunk, base, zone, whole):
    here = Here()
    put_together(here, kept, sides, row, whole)
    c, d = here.c, 1 - here.c

    picked = pick(here.by_row(sums[c, c], sums[d, c]), numbers_of(kept, NUMBERS + ORDER_TWO))
    redund = picked[:, SKEL:]
    values = dot_t(redund, block_of(whole, SOLVE_OWN))
    zone[...] = values
    other = pick(here.by_row(sums[d, d], sums[c, d]), numbers_of(whole, ORDER_SIDE * SKEL + ORDER_TWO))
    other = dot_t(other[:, SKEL:], block_of(whole, SOLVE_SIDE))
    for slot in range(4):
        chunk[slot, 0] = values
        chunk[slot, 1] = other
    interp = kept[INTERP_TWO : INTERP_TWO + HALF]
    gone = dot_t(redund, stacked(interp, interp))
    base[...] = jnp.where(here.own_half(), picked[:, :SKEL] - gone, 0.0)


def second_part_kernel(near_at, far_at, got, chunk, base, kept, whole, part):
    here = Here()
    out_x, out_y, out_xy = here.outside(got, (0,))
    out_side = jnp.where(here.edge_y, 0.0, got[here.across, 1])
    near = jnp.zeros(VALUES, jnp.float32)
    far = jnp.zeros(VALUES, jnp.float32)
    for a, value, beyond in ((0, chunk[0, 1], out_side), (1, chunk[0, 0], out_y), (2, out_x, out_xy)):
        own = kept[near_at + 2 * a * HALF : near_at + (2 * a + 1) * HALF]
        near = near + dot_t(value, stacked(own, own))
        far = far + dot_t(beyond, block_of(whole, far_at + a))
    part[...] = base[...] - jnp.where(here.own_half(), near, 0.0) - far


def third_kernel(sums, kept, whole, chunk, base, zone):
    here = Here()
    joined = lanes(sums[0, 0] + sums[1, 0], sums[0, 1] + sums[1, 1])
    picked = pick(joined, numbers_of(kept, NUMBERS + ORDER_THREE))
    redund = picked[:, SKEL:]
    values = dot_t(redund, block_of(whole, SOLVE_ALL))
    zone[...] = values
    for slot in range(4):
        chunk[slot] = values
    gone = dot_t(redund, four(kept[INTERP_THREE : INTERP_THREE + QUARTER]))
    gone = gone + dot_t(values, four(kept[COUPLE_THREE : COUPLE_THREE + QUARTER]))
    base[...] = jnp.where(here.own_quarter(), picked[:, :SKEL] - gone, 0.0)


def third_part_kernel(at, got, base, whole, part):
    here = Here(crossed=True)
    out_x, out_y, out_xy = here.outside(got)
    edge = jnp.where(here.same, out_x, out_y)
    part[...] = base[...] - (dot_t(out_xy, block_of(whole, at)) + dot_t(edge, block_of(whole, at + 1)))


def total(sums):
    return (sums[0, 0] + sums[0, 1]) + (sums[1, 0] + sums[1, 1])


def top_kernel(sums, kept, whole, zone, chunk, base):
    here = Here()
    values = dot_t(total(sums), block_of(whole, TOP_ALL))
    for slot in range(4):
        chunk[slot] = values
    gone = dot_t(values, four(kept[SPREAD_THREE : SPREAD_THREE + QUARTER]))
    base[...] = jnp.where(here.own_quarter(), zone[...] - gone, 0.0)


def back_three_kernel(sums, values, kept, zone, chunk, base):
    here = Here()
    final = place(lanes(values[0], total(sums)), numbers_of(kept, NUMBERS + ORDER_THREE))
    low, high = final[:, :SKEL], final[:, SKEL:]
    own = jnp.where(here.c == 0, low, high)
    other = jnp.where(here.c == 0, high, low)
    for slot in range(4):
        chunk[slot, 0] = own
        chunk[slot, 1] = other
    base[...] = jnp.where(here.own_half(), zone[...], 0.0)


def back_two_kernel(sums, values, kept, whole, chunk, boxes):
    here = Here()
    c, d = here.c, 1 - here.c
    own = lanes(values[0, 0], sums[0, c] + sums[1, c])
    own = place(own, numbers_of(kept, NUMBERS + ORDER_TWO))
    other = lanes(values[0, 1], sums[0, d] + sums[1, d])
    other = place(other, numbers_of(whole, ORDER_SIDE * SKEL + ORDER_TWO))

    def rows_of(final):
        low, high = final[:, :SKEL], final[:, SKEL:]
        return jnp.where(here.h == 0, low, high), jnp.where(here.h == 0, high, low)

    value, value_row = rows_of(own)
    value_side, value_diag = rows_of(other)
    boxes[0], boxes[1], boxes[2], boxes[3] = value, value_side, value_row, value_diag
    fill(here, boxes, chunk)


def last_kernel(got, boxes, kept, adjoint, shares):
    here = Here()
    rest = kept[ZONE_ONE:] - dot(around(here, got, boxes), kept[LIFT_ONE : LIFT_ONE + 9 * SKEL])
    final = place(lanes(boxes[0], rest), numbers_of(kept, NUMBERS + ORDER_ONE))
    result = lanes(dot(final, kept[LEAF : LEAF + BOX]), dot(final, kept[LEAF + BOX : LEAF + 2 * BOX]))
    adjoint[...] = result
    field = lanes(kept[FIELD : FIELD + COLS], kept[FIELD + COLS : FIELD + 2 * COLS])
    count = lax.axis_size("rhs")
    weight = jnp.sum(result * field, axis=0, keepdims=True) / (count * COLS)
    share = PANELS // count
    number = lax.broadcasted_iota(jnp.int32, (8 * count, BOX), 0)
    panel = jnp.where(number % 8 < share, number // 8 * share + number % 8, -1)
    inside = numbers_of(kept, NUMBERS + PANEL_OF) == panel
    sums = jnp.sum(jnp.where(inside, weight, 0.0), axis=1, keepdims=True)
    for r in range(count):
        shares[r] = jnp.broadcast_to(sums[8 * r : 8 * (r + 1)], (8, SKEL))


def spec(space, count):
    return [pl.BlockSpec(memory_space=space)] * count


def call(body, outs, *operands):
    outs = tuple(pltpu.VMEM(shape, jnp.float32) for shape in outs)
    result = pl.pallas_call(
        body,
        out_shape=outs,
        in_specs=spec(pltpu.VMEM, len(operands)),
        out_specs=tuple(spec(pltpu.VMEM, len(outs))),
        compiler_params=pltpu.CompilerParams(vmem_limit_bytes=VMEM_LIMIT),
    )(*[pltpu.with_memory_space_constraint(operand, pltpu.VMEM) for operand in operands])
    return result if len(outs) > 1 else result[0]


def start(arrays):
    outs = [
        pltpu.VMEM(shape, jnp.float32)
        for shape in (VALUES, VALUES, (5, *BLOCK), (3 * SKEL + 8, SKEL), (9 * SKEL, SKEL), KEPT)
    ]
    return pl.pallas_call(
        start_kernel,
        out_shape=tuple(outs),
        in_specs=spec(pl.ANY, len(NAMES)),
        out_specs=tuple(spec(pltpu.VMEM, len(outs))),
        scratch_shapes=[pltpu.VMEM(arrays[name].shape, arrays[name].dtype) for name in NAMES]
        + [pltpu.SemaphoreType.DMA((len(NAMES),))],
        compiler_params=pltpu.CompilerParams(vmem_limit_bytes=VMEM_LIMIT),
    )(*[pltpu.with_memory_space_constraint(arrays[name], pltpu.HBM) for name in NAMES])


def on_device(groups, *arguments):
    arrays = {}
    for name, value in zip(GIVEN, arguments):
        value = value[0] if value.ndim == 3 else value[0, 0]
        if value.shape[-1] in (HALF, QUARTER):
            value = jnp.swapaxes(value, -1, -2)
        arrays[name] = value

    def outside(chunk, crossed=False):
        members = groups.crossed if crossed else groups.shifted
        return lax.all_to_all(chunk, AXES, 0, 0, axis_index_groups=members)

    def shared(part):
        pair = lax.all_gather(part, AXES, axis_index_groups=groups.diagonal)
        return lax.all_gather(pair, AXES, axis_index_groups=groups.sibling)

    def from_row(blocks):
        return lax.ppermute(blocks, "by", [(i, i ^ 1) for i in range(lax.axis_size("by"))])

    zone_one, base, to_row, to_side, couple, kept = start(arrays)
    pair = lax.all_gather(zone_one, AXES, axis_index_groups=groups.diagonal)
    to_side = call(side_kernel, [SIDE], pair, to_side)
    sides = lax.all_gather(to_side, AXES, axis_index_groups=groups.sibling)
    chunk, boxes, to_row = call(
        row_kernel, [(4, 2, *VALUES), (4, *VALUES), (7, *BLOCK)], to_row, sides
    )
    row = from_row(to_row)
    part = call(first_kernel, [VALUES], outside(chunk), boxes, base, couple)

    one, two, three = [(4, *VALUES), VALUES, VALUES], [(4, 2, *VALUES), VALUES, VALUES], [VALUES]
    chunk, base, zone_two, whole = call(second_kernel, two + [WHOLE], shared(part), kept, sides, row)
    down_two = functools.partial(second_part_kernel, COUPLE_TWO, COUPLE_FAR)
    part = call(down_two, three, outside(chunk), chunk, base, kept, whole)
    chunk, base, zone_three = call(third_kernel, one, shared(part), kept, whole)
    down_three = functools.partial(third_part_kernel, COUPLE_ALL)
    part = call(down_three, three, outside(chunk, True), base, whole)
    chunk, base = call(top_kernel, one[:2], shared(part), kept, whole, zone_three)
    up_three = functools.partial(third_part_kernel, SPREAD_ALL)
    part = call(up_three, three, outside(chunk, True), base, whole)
    chunk, base = call(back_three_kernel, two[:2], shared(part), chunk, kept, zone_two)
    up_two = functools.partial(second_part_kernel, SPREAD_TWO, SPREAD_FAR)
    part = call(up_two, three, outside(chunk), chunk, base, kept, whole)
    chunk, boxes = call(back_two_kernel, [(4, 2, *VALUES), (4, *VALUES)], shared(part), chunk, kept, whole)
    count = lax.axis_size("rhs")
    adjoint, shares = call(last_kernel, [(COLS, BOX), (count, 8, SKEL)], outside(chunk), boxes, kept)
    shares = lax.all_to_all(shares, "rhs", 0, 0)
    gradient = jnp.sum(shares[:, : PANELS // count, 0], axis=0)
    return adjoint[None, None], gradient[None, None]


def solution(mesh):
    box = P("bx", "by")
    columns = P("bx", "by", "rhs", None)
    groups = Groups(mesh.shape["bx"], mesh.shape["by"], mesh.shape["rhs"])
    return jax.shard_map(
        functools.partial(on_device, groups),
        mesh=mesh,
        in_specs=(columns, columns) + (box,) * 23,
        out_specs=(columns, P("bx", "by", "rhs")),
        check_vma=False,
    )
```

time: 212 us -> 111 us (0.52)
  starting transfers between devices: 120 us -> 5.82 us
  blocking collectives: 8.71 us -> 92.3 us
  waiting for transfers between devices: 50.2 us -> 3.61 us
  other arithmetic: 12.3 us -> 0.63 us
  local copies, waits for them, and re-layouts: 11 us -> 0.6 us
  Pallas kernels: 0 us -> 6.38 us
  matrix products: 5.57 us -> 0 us
    ppermute x37 -> x1, starting transfers between devices: 120 us -> 1.92 us  [from_row(): lax.ppermute(blocks, 'by', [(i, i ^ 1) for i in range(lax.axis_size('by'))])]
    all_to_all x0 -> x6, blocking collectives: none -> 50.2 us  [outside(): return lax.all_to_all(chunk, AXES, 0, 0, axis_index_groups=members)]
    ppermute x37 -> x1, waiting for transfers between devices: 50.2 us -> 0.01 us  [from_row(): lax.ppermute(blocks, 'by', [(i, i ^ 1) for i in range(lax.axis_size('by'))])]
    all_gather x0 -> x12, blocking collectives: none -> 42.1 us  [the longest x5 19 us: shared(): pair = lax.all_gather(part, AXES, axis_index_groups=groups.diagonal)]
    sort x3 -> x0, other arithmetic: 10.2 us -> none  [placed_cols(): return jnp.take(values, jnp.argsort(order), axis=1)]
    unnamed x1 -> x0, blocking collectives: 8.71 us -> none
    pallas_call x0 -> x14, Pallas kernels: none -> 6.38 us  [the longest x13 3.94 us: call(): pl.pallas_call(body, out_shape=outs, in_specs=spec(pltpu.VMEM, len(operan...]
    dot_general x20 -> x0, matrix products: 5.57 us -> none  [the longest x12 2.03 us: matmul(): return jnp.matmul(left, right, precision=highest)]
  transfers between devices with their start and end apart: 37 -> 2, of which waited for: 23 -> 1; matrix products, arithmetic and copies ran while one was open for 4% -> 1% of each run, Pallas kernels for 0% -> 0%
where the time goes in v2:
time: 111 us; the launch traced here: 110 us
  blocking collectives  92.3 us (83%)
  Pallas kernels  6.38 us (6%)
  starting transfers between devices  5.82 us (5%)
  waiting for transfers between devices  3.61 us (3%)
    all_to_all x6, blocking collectives, outside(): return lax.all_to_all(chunk, AXES, 0, 0, axis_index_groups=members)  50.2 us
    all_gather x5, blocking collectives, shared(): pair = lax.all_gather(part, AXES, axis_index_groups=groups.diagonal)  19 us
    all_gather x5, blocking collectives, shared(): return lax.all_gather(pair, AXES, axis_index_groups=groups.sibling)  10.7 us
    all_gather x1, blocking collectives, on_device(): sides = lax.all_gather(to_side, AXES, axis_index_groups=groups.sibling)  7.36 us
    all_gather x1, blocking collectives, on_device(): pair = lax.all_gather(zone_one, AXES, axis_index_groups=groups.diagonal)  5.05 us
    pallas_call x13, Pallas kernels, call(): pl.pallas_call(body, out_shape=outs, in_specs=spec(pltpu.VMEM, len(operan...  3.94 us
    all_to_all x1, starting transfers between devices, on_device(): shares = lax.all_to_all(shares, 'rhs', 0, 0)  3.9 us
    all_to_all x1, waiting for transfers between devices, on_device(): shares = lax.all_to_all(shares, 'rhs', 0, 0)  3.61 us
  transfers between devices with their start and end apart: 2, of which 1 were waited for; matrix products, arithmetic and copies ran while one was open for 1% of the time, Pallas kernels for 0%

profile of v2, /device:TPU:1, one launch (start us, length us, event | category | flops | bytes accessed | tf_op | source)
XLA Modules:
  0.0 110.0 jit_solution(10280654340875645992)
XLA Ops:
  0.6 2.4 %shard_map.248 = (f32[16,128]{1,0:T(8,128)S(1)}, f32[16,128]{1,0:T(8,128)S(1)}, f32[5,128,128]{2,1,0:T(8,128)S(1)}, f32[392,128]{1,0:T(8,128)S(1)}, f32[1152,128]{1,0:T(8,128)S(1)}, /*index=5*/f32[2904,128]{1,0:T(8,128)S(1)}) custom-call(f32[16,256]{1,0:T(8,128)} %bitcast.89, f32[256,256]{1,0:T(8,128)} %bitcast.74, s32[1,256]{1,0:T(1,128)} %bitcast.95, ...), custom_call_target="tpu_custom_call" | custom-call | tf_op jit(solution)/shard_map/pallas_call | solution.py:548
  3.1 5.0 %all-gather = f32[32,128]{1,0:T(8,128)S(1)} all-gather(f32[16,128]{1,0:T(8,128)S(1)} %get-tuple-element.27), channel_id=2, replica_groups={{0,68},{1,69},{2,70},{3,71},{4,64},{5,65},{6,66},{7,67},{8,76},{9,77},{..., dimensions={0}, use_global_device_ids=true | all-gather | bytes 24576 | tf_op jit(solution)/shard_map/all_gather | solution.py:579
  8.2 7.4 %all-gather.1 = f32[848,128]{1,0:T(8,128)S(1)} all-gather(f32[424,128]{1,0:T(8,128)S(1)} %shard_map.249), channel_id=3, replica_groups={{0,64},{1,65},{2,66},{3,67},{4,68},{5,69},{6,70},{7,71},{8,72},{9,73},{..., dimensions={0}, use_global_device_ids=true | all-gather | bytes 651264 | tf_op jit(solution)/shard_map/all_gather | solution.py:581
  15.6 1.9 %collective-permute-start = (f32[7,128,128]{2,1,0:T(8,128)S(1)}, f32[7,128,128]{2,1,0:T(8,128)S(1)}, u32[]{:S(2)}, u32[]{:S(2)}) collective-permute-start(f32[7,128,128]{2,1,0:T(8,128)S(1)} %get-tuple-element.34), channel_id=1, source_target_pairs={{0,4},{4,0},{8,12},{12,8},{16,20},{20,16},{24,28},{28,24},{32,36},... | collective-permute-start | bytes 1376264 | tf_op jit(solution)/shard_map/ppermute | solution.py:576
  17.5 10.8 %all_to_all.35.got = f32[4,2,16,128]{3,2,1,0:T(8,128)S(1)} all-to-all(f32[4,2,16,128]{3,2,1,0:T(8,128)S(1)} %get-tuple-element.29), channel_id=1, replica_groups={{68,72,132,136},{196,200,260,264},{324,328,388,392},{4,8,5,9},{452,456,..., dimensions={0} | all-to-all | bytes 131072 | tf_op jit(solution)/shard_map/all_to_all | solution.py:569
  28.3 0.2 shard_map.251
  28.6 3.8 %all-gather.2 = f32[32,128]{1,0:T(8,128)S(1)} all-gather(f32[16,128]{1,0:T(8,128)S(1)} %shard_map.251), channel_id=4, replica_groups={{0,68},{1,69},{2,70},{3,71},{4,64},{5,65},{6,66},{7,67},{8,76},{9,77},{..., dimensions={0}, use_global_device_ids=true | all-gather | bytes 24576 | tf_op jit(solution)/shard_map/all_gather | solution.py:572
  32.3 2.4 %all-gather.3 = f32[4,16,128]{2,1,0:T(8,128)S(1)} all-gather(f32[2,16,128]{2,1,0:T(8,128)S(1)} %bitcast.81), channel_id=5, replica_groups={{0,64},{1,65},{2,66},{3,67},{4,68},{5,69},{6,70},{7,71},{8,72},{9,73},{..., dimensions={0}, use_global_device_ids=true | all-gather | bytes 49152 | tf_op jit(solution)/shard_map/all_gather | solution.py:573
  34.8 0.0 collective-permute-done.row
  34.8 0.4 shard_map.252
  35.2 8.0 %all_to_all.36.got = f32[4,2,16,128]{3,2,1,0:T(8,128)S(1)} all-to-all(f32[4,2,16,128]{3,2,1,0:T(8,128)S(1)} %get-tuple-element.35.chunk), channel_id=1, replica_groups={{68,72,132,136},{196,200,260,264},{324,328,388,392},{4,8,5,9},{452,456,..., dimensions={0} | all-to-all | bytes 131072 | tf_op jit(solution)/shard_map/all_to_all | solution.py:569
  43.2 0.3 shard_map.253
  43.5 3.8 %all-gather.4 = f32[32,128]{1,0:T(8,128)S(1)} all-gather(f32[16,128]{1,0:T(8,128)S(1)} %shard_map.253), channel_id=6, replica_groups={{0,68},{1,69},{2,70},{3,71},{4,64},{5,65},{6,66},{7,67},{8,76},{9,77},{..., dimensions={0}, use_global_device_ids=true | all-gather | bytes 24576 | tf_op jit(solution)/shard_map/all_gather | solution.py:572
  47.3 2.3 %all-gather.5 = f32[4,16,128]{2,1,0:T(8,128)S(1)} all-gather(f32[2,16,128]{2,1,0:T(8,128)S(1)} %bitcast.82), channel_id=7, replica_groups={{0,64},{1,65},{2,66},{3,67},{4,68},{5,69},{6,70},{7,71},{8,72},{9,73},{..., dimensions={0}, use_global_device_ids=true | all-gather | bytes 49152 | tf_op jit(solution)/shard_map/all_gather | solution.py:573
  49.6 0.4 shard_map.254
  50.0 8.0 %all_to_all.37.got = f32[4,16,128]{2,1,0:T(8,128)S(1)} all-to-all(f32[4,16,128]{2,1,0:T(8,128)S(1)} %get-tuple-element.38), channel_id=1, replica_groups={{68,8,132,200},{196,136,260,328},{324,264,388,456},{4,72,5,73},{452,392..., dimensions={0} | all-to-all | bytes 65536 | tf_op jit(solution)/shard_map/all_to_all | solution.py:569
  57.9 0.2 shard_map.255
  58.1 3.8 %all-gather.6 = f32[32,128]{1,0:T(8,128)S(1)} all-gather(f32[16,128]{1,0:T(8,128)S(1)} %shard_map.255), channel_id=8, replica_groups={{0,68},{1,69},{2,70},{3,71},{4,64},{5,65},{6,66},{7,67},{8,76},{9,77},{..., dimensions={0}, use_global_device_ids=true | all-gather | bytes 24576 | tf_op jit(solution)/shard_map/all_gather | solution.py:572
  61.9 1.9 %all-gather.7 = f32[4,16,128]{2,1,0:T(8,128)S(1)} all-gather(f32[2,16,128]{2,1,0:T(8,128)S(1)} %bitcast.83), channel_id=9, replica_groups={{0,64},{1,65},{2,66},{3,67},{4,68},{5,69},{6,70},{7,71},{8,72},{9,73},{..., dimensions={0}, use_global_device_ids=true | all-gather | bytes 49152 | tf_op jit(solution)/shard_map/all_gather | solution.py:573
  63.8 0.3 shard_map.256
  64.0 7.7 %all_to_all.38.got = f32[4,16,128]{2,1,0:T(8,128)S(1)} all-to-all(f32[4,16,128]{2,1,0:T(8,128)S(1)} %get-tuple-element.41.values), channel_id=1, replica_groups={{68,8,132,200},{196,136,260,328},{324,264,388,456},{4,72,5,73},{452,392..., dimensions={0} | all-to-all | bytes 65536 | tf_op jit(solution)/shard_map/all_to_all | solution.py:569
  71.7 0.2 shard_map.257
  71.9 3.8 %all-gather.8 = f32[32,128]{1,0:T(8,128)S(1)} all-gather(f32[16,128]{1,0:T(8,128)S(1)} %shard_map.257), channel_id=10, replica_groups={{0,68},{1,69},{2,70},{3,71},{4,64},{5,65},{6,66},{7,67},{8,76},{9,77},{..., dimensions={0}, use_global_device_ids=true | all-gather | bytes 24576 | tf_op jit(solution)/shard_map/all_gather | solution.py:572
  75.7 1.9 %all-gather.9 = f32[4,16,128]{2,1,0:T(8,128)S(1)} all-gather(f32[2,16,128]{2,1,0:T(8,128)S(1)} %bitcast.84), channel_id=11, replica_groups={{0,64},{1,65},{2,66},{3,67},{4,68},{5,69},{6,70},{7,71},{8,72},{9,73},{..., dimensions={0}, use_global_device_ids=true | all-gather | bytes 49152 | tf_op jit(solution)/shard_map/all_gather | solution.py:573
  77.6 0.2 shard_map.258
  77.8 7.7 %all_to_all.39.got = f32[4,2,16,128]{3,2,1,0:T(8,128)S(1)} all-to-all(f32[4,2,16,128]{3,2,1,0:T(8,128)S(1)} %get-tuple-element.44.chunk.values), channel_id=1, replica_groups={{68,72,132,136},{196,200,260,264},{324,328,388,392},{4,8,5,9},{452,456,..., dimensions={0} | all-to-all | bytes 131072 | tf_op jit(solution)/shard_map/all_to_all | solution.py:569
  85.5 0.3 shard_map.259
  85.8 3.8 %all-gather.10 = f32[32,128]{1,0:T(8,128)S(1)} all-gather(f32[16,128]{1,0:T(8,128)S(1)} %shard_map.259), channel_id=12, replica_groups={{0,68},{1,69},{2,70},{3,71},{4,64},{5,65},{6,66},{7,67},{8,76},{9,77},{..., dimensions={0}, use_global_device_ids=true | all-gather | bytes 24576 | tf_op jit(solution)/shard_map/all_gather | solution.py:572
  89.6 2.3 %all-gather.11 = f32[4,16,128]{2,1,0:T(8,128)S(1)} all-gather(f32[2,16,128]{2,1,0:T(8,128)S(1)} %bitcast.85), channel_id=13, replica_groups={{0,64},{1,65},{2,66},{3,67},{4,68},{5,69},{6,70},{7,71},{8,72},{9,73},{..., dimensions={0}, use_global_device_ids=true | all-gather | bytes 49152 | tf_op jit(solution)/shard_map/all_gather | solution.py:573
  91.9 0.2 shard_map.260
  92.1 8.0 %all_to_all.40.got = f32[4,2,16,128]{3,2,1,0:T(8,128)S(1)} all-to-all(f32[4,2,16,128]{3,2,1,0:T(8,128)S(1)} %get-tuple-element.46), channel_id=1, replica_groups={{68,72,132,136},{196,200,260,264},{324,328,388,392},{4,8,5,9},{452,456,..., dimensions={0} | all-to-all | bytes 131072 | tf_op jit(solution)/shard_map/all_to_all | solution.py:569
  100.0 1.2 %shard_map.261 = (f32[16,256]{1,0:T(8,128)S(1)}, f32[4,8,128]{2,1,0:T(8,128)}) custom-call(f32[4,2,16,128]{3,2,1,0:T(8,128)S(1)} %all_to_all.40.got, f32[4,16,128]{2,1,0:T(8,128)S(1)} %get-tuple-element.47.boxes, f32[2904,128]{1,0:T(8,128)S(1)} %get-tuple-element.33.kept), custom_call_target="tpu_custom_call" | custom-call | tf_op jit(solution)/shard_map/pallas_call | solution.py:533
  101.3 3.9 %all-to-all-start.6 = ((f32[4,8,128]{2,1,0:T(8,128)}), f32[4,8,128]{2,1,0:T(8,128)S(1)}, u32[]{:S(2)}, u32[]{:S(2)}) async-start(f32[4,8,128]{2,1,0:T(8,128)} %get-tuple-element.49), calls=%async_computation.6 | async-start | bytes 32768 | tf_op jit(solution)/shard_map/all_to_all | solution.py:604
  105.2 0.6 copy.27
  105.8 3.6 %all-to-all-done.6 = f32[4,8,128]{2,1,0:T(8,128)S(1)} async-done(((f32[4,8,128]{2,1,0:T(8,128)}), f32[4,8,128]{2,1,0:T(8,128)S(1)}, u32[]{:S(2)}, u32[]{:S(2)}) %all-to-all-start.6) | async-done | bytes 16416 | tf_op jit(solution)/shard_map/all_to_all | solution.py:604
  109.4 0.6 slice_reduce_fusion
  (2 shorter events, 0.1 us)
Async XLA Ops:
  15.6 19.2 %collective-permute-start = (f32[7,128,128]{2,1,0:T(8,128)S(1)}, f32[7,128,128]{2,1,0:T(8,128)S(1)}, u32[]{:S(2)}, u32[]{:S(2)}) collective-permute-start(f32[7,128,128]{2,1,0:T(8,128)S(1)} %get-tuple-element.34), channel_id=1, source_target_pairs={{0,4},{4,0},{8,12},{12,8},{16,20},{20,16},{24,28},{28,24},{32,36},... | collective-permute-start | bytes 1376264 | tf_op jit(solution)/shard_map/ppermute | solution.py:576
  101.3 8.1 %all-to-all-start.6 = ((f32[4,8,128]{2,1,0:T(8,128)}), f32[4,8,128]{2,1,0:T(8,128)S(1)}, u32[]{:S(2)}, u32[]{:S(2)}) async-start(f32[4,8,128]{2,1,0:T(8,128)} %get-tuple-element.49), calls=%async_computation.6 | async-start | bytes 32768 | tf_op jit(solution)/shard_map/all_to_all | solution.py:604

commit v3 on v2

--- a/solution.py
+++ b/solution.py
@@ -70,31 +70,33 @@
         every = [(i, j, r) for i in range(size_x) for j in range(size_y) for r in range(size_r)]
         self.sibling = [[place(i, j, r), place(i + 1, j, r)] for i, j, r in every if i % 2 == 0]
         self.diagonal = [[place(i, j, r), place(i + 1, j ^ 1, r)] for i, j, r in every if i % 2 == 0]
-        self.shifted = []
-        self.crossed = []
+        self.shifted, self.crossed = [], []
+        last = size_x - 1
         for j in range(1, size_y, 2):
-            after = (j + 1) % size_y
             for r in range(size_r):
-                for i in range(1, size_x - 1, 2):
-                    self.shifted.append(
-                        [place(i, j, r), place(i, after, r), place(i + 1, j, r), place(i + 1, after, r)]
-                    )
-                    self.crossed.append(
-                        [place(i, j, r), place(i - 1, after, r), place(i + 1, j, r), place(i + 2, after, r)]
-                    )
-                if r % 2 == 0:
-                    for i in (0, size_x - 1):
-                        self.shifted.append(
-                            [place(i, j, r), place(i, after, r), place(i, j, r + 1), place(i, after, r + 1)]
-                        )
-                        self.crossed.append(
-                            [
-                                place(i, j, r),
-                                place(i ^ 1, after, r),
-                                place(i, j, r + 1),
-                                place(i ^ 1, after, r + 1),
-                            ]
-                        )
+                for i in range(1, last, 2):
+                    shifted, crossed = [(i, j), (i + 1, j)], [(i, j), (i + 1, j)]
+                    if j + 1 < size_y:
+                        shifted += [(i, j + 1), (i + 1, j + 1)]
+                        crossed += [(i - 1, j + 1), (i + 2, j + 1)]
+                        self.shifted.append([place(*at, r) for at in shifted])
+                        self.crossed.append([place(*at, r) for at in crossed])
+                    elif r % 2 == 0:
+                        low = [(i, 0), (i + 1, 0)], [(i - 1, 0), (i + 2, 0)]
+                        for groups, members in (
+                            (self.shifted, shifted),
+                            (self.crossed, crossed),
+                            (self.shifted, low[0]),
+                            (self.crossed, low[1]),
+                        ):
+                            groups.append([place(*at, r + n) for n in (0, 1) for at in members])
+                for i in (0, last):
+                    for groups, k in ((self.shifted, i), (self.crossed, i ^ 1)):
+                        if j + 1 < size_y and r % 2 == 0:
+                            groups.append([place(*at, r + n) for at in ((i, j), (k, j + 1)) for n in (0, 1)])
+                        elif j + 1 == size_y and r % 4 == 0:
+                            groups.append([place(i, j, r + n) for n in range(4)])
+                            groups.append([place(k, 0, r + n) for n in range(4)])
 
 
 class Here:
@@ -106,11 +108,12 @@
         self.edge_x = ((chip == 0) & (side == 0)) | ((chip == lax.axis_size("bx") - 2) & (side == 1))
         self.edge_y = (y == 0) | (y == lax.axis_size("by") - 1)
         slot_x = jnp.where(self.edge_x, lax.rem(r, 2), 1 - side)
-        slot_y = 1 - self.h
+        shared = jnp.where(self.edge_x, lax.rem(r, 4) // 2, lax.rem(r, 2))
+        slot_y = jnp.where(self.edge_y, shared, 1 - self.h)
         self.slot_y = slot_y
-        self.along = 2 * (1 - slot_x) + slot_y
-        self.across = 2 * slot_x + 1 - slot_y
-        self.corner = 2 * (1 - slot_x) + 1 - slot_y
+        self.along = 2 * slot_y + 1 - slot_x
+        self.across = 2 * (1 - slot_y) + slot_x
+        self.corner = 2 * (1 - slot_y) + 1 - slot_x
         side_x = (2 - 2 * side, 1, 2 * side)
         side_y = (2 - 2 * self.h, 1, 2 * self.h)
         self.block = [[3 * a + b for b in side_y] for a in side_x]
@@ -343,7 +346,7 @@
 def fill(here, boxes, chunk):
     for slot in range(4):
         chunk[slot, 0] = boxes[0]
-        chunk[slot, 1] = jnp.where(here.slot_y == slot % 2, boxes[2], boxes[1])
+        chunk[slot, 1] = jnp.where(here.slot_y == slot // 2, boxes[2], boxes[1])
 
 
 def around(here, got, boxes):
@@ -516,12 +519,21 @@
     count = lax.axis_size("rhs")
     weight = jnp.sum(result * field, axis=0, keepdims=True) / (count * COLS)
     share = PANELS // count
-    number = lax.broadcasted_iota(jnp.int32, (8 * count, BOX), 0)
-    panel = jnp.where(number % 8 < share, number // 8 * share + number % 8, -1)
-    inside = numbers_of(kept, NUMBERS + PANEL_OF) == panel
-    sums = jnp.sum(jnp.where(inside, weight, 0.0), axis=1, keepdims=True)
+    number = lax.broadcasted_iota(jnp.int32, (SKEL, BOX), 0)
+    panels = numbers_of(kept, NUMBERS + PANEL_OF)
+    weight = jnp.broadcast_to(weight, (COLS, BOX))
     for r in range(count):
-        shares[r] = jnp.broadcast_to(sums[8 * r : 8 * (r + 1)], (8, SKEL))
+        inside = (number < share) & (panels == number + r * share)
+        inside = jnp.where(inside, 1.0, 0.0).astype(jnp.bfloat16)
+        shares[r] = dims(weight, (inside,), 1)[:8]
+
+
+def end_kernel(adjoint, shares, adjoint_out, gradient_out):
+    adjoint_out[...] = adjoint[...]
+    total = shares[0, 0:1] + shares[1, 0:1]
+    for r in range(2, shares.shape[0]):
+        total = total + shares[r, 0:1]
+    gradient_out[...] = total[:, : gradient_out.shape[1]]
 
 
 def spec(space, count):
@@ -602,8 +614,17 @@
     count = lax.axis_size("rhs")
     adjoint, shares = call(last_kernel, [(COLS, BOX), (count, 8, SKEL)], outside(chunk), boxes, kept)
     shares = lax.all_to_all(shares, "rhs", 0, 0)
-    gradient = jnp.sum(shares[:, : PANELS // count, 0], axis=0)
-    return adjoint[None, None], gradient[None, None]
+    adjoint, gradient = pl.pallas_call(
+        end_kernel,
+        out_shape=(
+            jax.ShapeDtypeStruct((COLS, BOX), jnp.float32),
+            jax.ShapeDtypeStruct((1, PANELS // count), jnp.float32),
+        ),
+        in_specs=spec(pltpu.VMEM, 2),
+        out_specs=tuple(spec(pltpu.VMEM, 2)),
+        compiler_params=pltpu.CompilerParams(vmem_limit_bytes=VMEM_LIMIT),
+    )(*[pltpu.with_memory_space_constraint(operand, pltpu.VMEM) for operand in (adjoint, shares)])
+    return adjoint[None, None], gradient[None]
 
 
 def solution(mesh):

time: 111 us -> 108 us (0.973)
  the two profiles are of different devices: /device:TPU:1 before, /device:TPU:96 now
where the time goes in v3:
time: 108 us; the launch traced here: 107 us
  blocking collectives  98.2 us (91%)
  Pallas kernels  6.44 us (6%)
  starting transfers between devices  1.95 us (2%)
    all_to_all x6, blocking collectives, outside(): return lax.all_to_all(chunk, AXES, 0, 0, axis_index_groups=members)  54.8 us
    all_gather x5, blocking collectives, shared(): pair = lax.all_gather(part, AXES, axis_index_groups=groups.diagonal)  19 us
    all_to_all x1, blocking collectives, on_device(): shares = lax.all_to_all(shares, 'rhs', 0, 0)  9.35 us
    all_gather x5, blocking collectives, shared(): return lax.all_gather(pair, AXES, axis_index_groups=groups.sibling)  9.09 us
    all_gather x1, blocking collectives, on_device(): pair = lax.all_gather(zone_one, AXES, axis_index_groups=groups.diagonal)  3.86 us
    pallas_call x13, Pallas kernels, call(): pl.pallas_call(body, out_shape=outs, in_specs=spec(pltpu.VMEM, len(operan...  3.39 us
    pallas_call x1, Pallas kernels, start(): pl.pallas_call(start_kernel, out_shape=tuple(outs), in_specs=spec(pl.ANY,...  2.44 us
  transfers between devices with their start and end apart: 1, of which 0 were waited for; matrix products, arithmetic and copies ran while one was open for 0% of the time, Pallas kernels for 0%

profile of v3, /device:TPU:96, one launch (start us, length us, event | category | flops | bytes accessed | tf_op | source)
XLA Modules:
  0.0 107.3 jit_solution(4781705356329043622)
XLA Ops:
  0.6 2.4 %shard_map.248 = (f32[16,128]{1,0:T(8,128)S(1)}, f32[16,128]{1,0:T(8,128)S(1)}, f32[5,128,128]{2,1,0:T(8,128)S(1)}, f32[392,128]{1,0:T(8,128)S(1)}, f32[1152,128]{1,0:T(8,128)S(1)}, /*index=5*/f32[2904,128]{1,0:T(8,128)S(1)}) custom-call(f32[16,256]{1,0:T(8,128)} %bitcast.88, f32[256,256]{1,0:T(8,128)} %bitcast.73, s32[1,256]{1,0:T(1,128)} %bitcast.94, ...), custom_call_target="tpu_custom_call" | custom-call | tf_op jit(solution)/shard_map/pallas_call | solution.py:560
  3.1 3.9 %all-gather = f32[32,128]{1,0:T(8,128)S(1)} all-gather(f32[16,128]{1,0:T(8,128)S(1)} %get-tuple-element.29), channel_id=2, replica_groups={{0,68},{1,69},{2,70},{3,71},{4,64},{5,65},{6,66},{7,67},{8,76},{9,77},{..., dimensions={0}, use_global_device_ids=true | all-gather | bytes 24576 | tf_op jit(solution)/shard_map/all_gather | solution.py:591
  7.0 2.1 %all-gather.1 = f32[848,128]{1,0:T(8,128)S(1)} all-gather(f32[424,128]{1,0:T(8,128)S(1)} %shard_map.249), channel_id=3, replica_groups={{0,64},{1,65},{2,66},{3,67},{4,68},{5,69},{6,70},{7,71},{8,72},{9,73},{..., dimensions={0}, use_global_device_ids=true | all-gather | bytes 651264 | tf_op jit(solution)/shard_map/all_gather | solution.py:593
  9.1 1.9 %collective-permute-start = (f32[7,128,128]{2,1,0:T(8,128)S(1)}, f32[7,128,128]{2,1,0:T(8,128)S(1)}, u32[]{:S(2)}, u32[]{:S(2)}) collective-permute-start(f32[7,128,128]{2,1,0:T(8,128)S(1)} %get-tuple-element.36), channel_id=1, source_target_pairs={{0,4},{4,0},{8,12},{12,8},{16,20},{20,16},{24,28},{28,24},{32,36},... | collective-permute-start | bytes 1376264 | tf_op jit(solution)/shard_map/ppermute | solution.py:588
  11.1 13.1 %all_to_all.35.got = f32[4,2,16,128]{3,2,1,0:T(8,128)S(1)} all-to-all(f32[4,2,16,128]{3,2,1,0:T(8,128)S(1)} %get-tuple-element.31), channel_id=1, replica_groups={{68,132,72,136},{196,260,200,264},{324,388,328,392},{4,5,8,9},{452,453,..., dimensions={0} | all-to-all | bytes 131072 | tf_op jit(solution)/shard_map/all_to_all | solution.py:581
  24.2 0.2 shard_map.251
  24.5 3.8 %all-gather.2 = f32[32,128]{1,0:T(8,128)S(1)} all-gather(f32[16,128]{1,0:T(8,128)S(1)} %shard_map.251), channel_id=4, replica_groups={{0,68},{1,69},{2,70},{3,71},{4,64},{5,65},{6,66},{7,67},{8,76},{9,77},{..., dimensions={0}, use_global_device_ids=true | all-gather | bytes 24576 | tf_op jit(solution)/shard_map/all_gather | solution.py:584
  28.3 1.8 %all-gather.3 = f32[4,16,128]{2,1,0:T(8,128)S(1)} all-gather(f32[2,16,128]{2,1,0:T(8,128)S(1)} %bitcast.80), channel_id=5, replica_groups={{0,64},{1,65},{2,66},{3,67},{4,68},{5,69},{6,70},{7,71},{8,72},{9,73},{..., dimensions={0}, use_global_device_ids=true | all-gather | bytes 49152 | tf_op jit(solution)/shard_map/all_gather | solution.py:585
  30.1 0.0 collective-permute-done.row
  30.1 0.4 shard_map.252
  30.5 8.4 %all_to_all.36.got = f32[4,2,16,128]{3,2,1,0:T(8,128)S(1)} all-to-all(f32[4,2,16,128]{3,2,1,0:T(8,128)S(1)} %get-tuple-element.37.chunk), channel_id=1, replica_groups={{68,132,72,136},{196,260,200,264},{324,388,328,392},{4,5,8,9},{452,453,..., dimensions={0} | all-to-all | bytes 131072 | tf_op jit(solution)/shard_map/all_to_all | solution.py:581
  39.0 0.3 shard_map.253
  39.3 3.8 %all-gather.4 = f32[32,128]{1,0:T(8,128)S(1)} all-gather(f32[16,128]{1,0:T(8,128)S(1)} %shard_map.253), channel_id=6, replica_groups={{0,68},{1,69},{2,70},{3,71},{4,64},{5,65},{6,66},{7,67},{8,76},{9,77},{..., dimensions={0}, use_global_device_ids=true | all-gather | bytes 24576 | tf_op jit(solution)/shard_map/all_gather | solution.py:584
  43.1 1.8 %all-gather.5 = f32[4,16,128]{2,1,0:T(8,128)S(1)} all-gather(f32[2,16,128]{2,1,0:T(8,128)S(1)} %bitcast.81), channel_id=7, replica_groups={{0,64},{1,65},{2,66},{3,67},{4,68},{5,69},{6,70},{7,71},{8,72},{9,73},{..., dimensions={0}, use_global_device_ids=true | all-gather | bytes 49152 | tf_op jit(solution)/shard_map/all_gather | solution.py:585
  44.9 0.4 shard_map.254
  45.3 8.5 %all_to_all.37.got = f32[4,16,128]{2,1,0:T(8,128)S(1)} all-to-all(f32[4,16,128]{2,1,0:T(8,128)S(1)} %get-tuple-element.40), channel_id=1, replica_groups={{68,132,8,200},{196,260,136,328},{324,388,264,456},{4,5,72,73},{452,453..., dimensions={0} | all-to-all | bytes 65536 | tf_op jit(solution)/shard_map/all_to_all | solution.py:581
  53.8 0.2 shard_map.255
  53.9 3.8 %all-gather.6 = f32[32,128]{1,0:T(8,128)S(1)} all-gather(f32[16,128]{1,0:T(8,128)S(1)} %shard_map.255), channel_id=8, replica_groups={{0,68},{1,69},{2,70},{3,71},{4,64},{5,65},{6,66},{7,67},{8,76},{9,77},{..., dimensions={0}, use_global_device_ids=true | all-gather | bytes 24576 | tf_op jit(solution)/shard_map/all_gather | solution.py:584
  57.7 1.8 %all-gather.7 = f32[4,16,128]{2,1,0:T(8,128)S(1)} all-gather(f32[2,16,128]{2,1,0:T(8,128)S(1)} %bitcast.82), channel_id=9, replica_groups={{0,64},{1,65},{2,66},{3,67},{4,68},{5,69},{6,70},{7,71},{8,72},{9,73},{..., dimensions={0}, use_global_device_ids=true | all-gather | bytes 49152 | tf_op jit(solution)/shard_map/all_gather | solution.py:585
  59.5 0.3 shard_map.256
  59.8 7.8 %all_to_all.38.got = f32[4,16,128]{2,1,0:T(8,128)S(1)} all-to-all(f32[4,16,128]{2,1,0:T(8,128)S(1)} %get-tuple-element.43.values), channel_id=1, replica_groups={{68,132,8,200},{196,260,136,328},{324,388,264,456},{4,5,72,73},{452,453..., dimensions={0} | all-to-all | bytes 65536 | tf_op jit(solution)/shard_map/all_to_all | solution.py:581
  67.6 0.2 shard_map.257
  67.8 3.8 %all-gather.8 = f32[32,128]{1,0:T(8,128)S(1)} all-gather(f32[16,128]{1,0:T(8,128)S(1)} %shard_map.257), channel_id=10, replica_groups={{0,68},{1,69},{2,70},{3,71},{4,64},{5,65},{6,66},{7,67},{8,76},{9,77},{..., dimensions={0}, use_global_device_ids=true | all-gather | bytes 24576 | tf_op jit(solution)/shard_map/all_gather | solution.py:584
  71.6 1.8 %all-gather.9 = f32[4,16,128]{2,1,0:T(8,128)S(1)} all-gather(f32[2,16,128]{2,1,0:T(8,128)S(1)} %bitcast.83), channel_id=11, replica_groups={{0,64},{1,65},{2,66},{3,67},{4,68},{5,69},{6,70},{7,71},{8,72},{9,73},{..., dimensions={0}, use_global_device_ids=true | all-gather | bytes 49152 | tf_op jit(solution)/shard_map/all_gather | solution.py:585
  73.4 0.2 shard_map.258
  73.6 8.5 %all_to_all.39.got = f32[4,2,16,128]{3,2,1,0:T(8,128)S(1)} all-to-all(f32[4,2,16,128]{3,2,1,0:T(8,128)S(1)} %get-tuple-element.46.chunk.values), channel_id=1, replica_groups={{68,132,72,136},{196,260,200,264},{324,388,328,392},{4,5,8,9},{452,453,..., dimensions={0} | all-to-all | bytes 131072 | tf_op jit(solution)/shard_map/all_to_all | solution.py:581
  82.1 0.3 shard_map.259
  82.4 3.8 %all-gather.10 = f32[32,128]{1,0:T(8,128)S(1)} all-gather(f32[16,128]{1,0:T(8,128)S(1)} %shard_map.259), channel_id=12, replica_groups={{0,68},{1,69},{2,70},{3,71},{4,64},{5,65},{6,66},{7,67},{8,76},{9,77},{..., dimensions={0}, use_global_device_ids=true | all-gather | bytes 24576 | tf_op jit(solution)/shard_map/all_gather | solution.py:584
  86.2 1.8 %all-gather.11 = f32[4,16,128]{2,1,0:T(8,128)S(1)} all-gather(f32[2,16,128]{2,1,0:T(8,128)S(1)} %bitcast.84), channel_id=13, replica_groups={{0,64},{1,65},{2,66},{3,67},{4,68},{5,69},{6,70},{7,71},{8,72},{9,73},{..., dimensions={0}, use_global_device_ids=true | all-gather | bytes 49152 | tf_op jit(solution)/shard_map/all_gather | solution.py:585
  88.0 0.2 shard_map.260
  88.2 8.4 %all_to_all.40.got = f32[4,2,16,128]{3,2,1,0:T(8,128)S(1)} all-to-all(f32[4,2,16,128]{3,2,1,0:T(8,128)S(1)} %get-tuple-element.48), channel_id=1, replica_groups={{68,132,72,136},{196,260,200,264},{324,388,328,392},{4,5,8,9},{452,453,..., dimensions={0} | all-to-all | bytes 131072 | tf_op jit(solution)/shard_map/all_to_all | solution.py:581
  96.7 0.7 shard_map.261
  97.3 9.4 %all_to_all.41.shares = f32[4,8,128]{2,1,0:T(8,128)S(1)} all-to-all(f32[4,8,128]{2,1,0:T(8,128)S(1)} %get-tuple-element.51), channel_id=1, replica_groups=mesh['bx'=8,'by'=16,'rhs'=4] {'rhs'}, dimensions={0} | all-to-all | bytes 32768 | tf_op jit(solution)/shard_map/all_to_all | solution.py:616
  106.7 0.6 shard_map.262
  (2 shorter events, 0.1 us)
Async XLA Ops:
  9.1 20.9 %collective-permute-start = (f32[7,128,128]{2,1,0:T(8,128)S(1)}, f32[7,128,128]{2,1,0:T(8,128)S(1)}, u32[]{:S(2)}, u32[]{:S(2)}) collective-permute-start(f32[7,128,128]{2,1,0:T(8,128)S(1)} %get-tuple-element.36), channel_id=1, source_target_pairs={{0,4},{4,0},{8,12},{12,8},{16,20},{20,16},{24,28},{28,24},{32,36},... | collective-permute-start | bytes 1376264 | tf_op jit(solution)/shard_map/ppermute | solution.py:588

commit v4 on v3

--- a/solution.py
+++ b/solution.py
@@ -153,8 +153,6 @@
     "solve_one",
     "interp_one",
     "near_one",
-    "couple_one",
-    "spread_one",
     "couple_two",
     "spread_two",
     "couple_three",
@@ -201,8 +199,8 @@
     "top_three",
 )
 
-LIFT_ONE = 0
-LEAF = LIFT_ONE + 9 * SKEL
+BACK_ONE = 0
+LEAF = BACK_ONE + SKEL
 COUPLE_TWO = LEAF + 2 * BOX
 SPREAD_TWO = COUPLE_TWO + 6 * HALF
 INTERP_TWO = SPREAD_TWO + 6 * HALF
@@ -215,7 +213,8 @@
 NUMBERS = TOP_THREE + QUARTER
 FIELD = NUMBERS + 8
 ZONE_ONE = FIELD + 2 * COLS
-KEPT = (ZONE_ONE + COLS, SKEL)
+NEAR = ZONE_ONE + COLS
+KEPT = (NEAR + 16, SKEL)
 ORDER_ONE, ORDER_TWO, ORDER_THREE, PANEL_OF = range(0, 8, 2)
 
 SOLVE_OWN, SOLVE_SIDE, SOLVE_ALL, TOP_ALL, COUPLE_ALL, SPREAD_ALL = 0, 1, 2, 3, 4, 6
@@ -237,8 +236,8 @@
 def start_kernel(*refs):
     count = len(NAMES)
     source = dict(zip(NAMES, refs[:count]))
-    zone, base, row_out, side_out, couple, kept = refs[count : count + 6]
-    held = dict(zip(NAMES, refs[count + 6 : -1]))
+    zone, base, row_out, side_out, kept = refs[count : count + 5]
+    held = dict(zip(NAMES, refs[count + 5 : -1]))
     sems = refs[-1]
     here = Here()
     copies = {name: pltpu.make_async_copy(source[name], held[name], sems.at[i]) for i, name in enumerate(NAMES)}
@@ -257,19 +256,12 @@
     redund = picked[:, SKEL:]
     values = dot(redund, read("solve_one"))
     zone[...] = values
-    kept[ZONE_ONE:] = values
+    kept[ZONE_ONE:NEAR] = values
     base[...] = picked[:, :SKEL] - dot(redund, read("interp_one"))
     spots = lax.broadcasted_iota(jnp.int32, (16, 9), 0) == lax.broadcasted_iota(jnp.int32, (16, 9), 1)
     near = jnp.where(spots, read("near_one").astype(jnp.float32), 0.0)
-    near = jnp.broadcast_to(jnp.sum(near, axis=1, keepdims=True), VALUES)
-    number = lax.broadcasted_iota(jnp.int32, VALUES, 0)
-
-    def scaled(name, a, b):
-        n = here.block[a][b]
-        weight = jnp.sum(jnp.where(number == n, near, 0.0), axis=0, keepdims=True)
-        return weight * held[name][n]
-
-    for name in NAMES[NAMES.index("couple_one") :]:
+    kept[NEAR:] = jnp.broadcast_to(jnp.sum(near, axis=1, keepdims=True), VALUES)
+    for name in NAMES[NAMES.index("couple_two") :]:
         copies[name].wait()
     for out, start in ((row_out.at[0], 0), (side_out, 0)):
         out[start : start + HALF] = held["solve_two"][...]
@@ -295,12 +287,6 @@
         row_out[2 + a, :HALF] = held["couple_two"][n]
         row_out[2 + a, HALF:] = held["spread_two"][n]
     for a in range(3):
-        for b in range(3):
-            at = (3 * a + b) * SKEL
-            couple[at : at + SKEL] = scaled("couple_one", a, b)
-            at = LIFT_ONE + at
-            block = scaled("spread_one", a, b)
-            kept[at : at + SKEL] = block + held["back_one"][...] if a == b == 1 else block
         for b in (1, 2):
             n = here.block[a][b]
             at = COUPLE_TWO + (2 * a + b - 1) * HALF
@@ -333,6 +319,7 @@
         kept[NUMBERS + row : NUMBERS + row + 1] = numbers[:, :SKEL]
         kept[NUMBERS + row + 1 : NUMBERS + row + 2] = numbers[:, SKEL:]
     side_out[3 * SKEL :] = kept[NUMBERS : NUMBERS + 8]
+    kept[BACK_ONE : BACK_ONE + SKEL] = held["back_one"][...]
     field = dot(held["forward"][...], held["derivative"][...])
     kept[FIELD : FIELD + COLS] = field[:, :SKEL]
     kept[FIELD + COLS : FIELD + 2 * COLS] = field[:, SKEL:]
@@ -349,11 +336,14 @@
         chunk[slot, 1] = jnp.where(here.slot_y == slot // 2, boxes[2], boxes[1])
 
 
-def around(here, got, boxes):
+def around(here, got, boxes, kept):
     out_x, out_y, out_xy = here.outside(got, (0,))
     out_x_row = jnp.where(here.edge_x, 0.0, got[here.along, 1])
     out_y_side = jnp.where(here.edge_y, 0.0, got[here.across, 1])
-    return lanes(boxes[3], boxes[1], out_y_side, boxes[2], boxes[0], out_y, out_x_row, out_x, out_xy)
+    grid = ((boxes[3], boxes[1], out_y_side), (boxes[2], boxes[0], out_y), (out_x_row, out_x, out_xy))
+    grid = [[jnp.where(here.c == 1, grid[a][b], grid[2 - a][b]) for b in range(3)] for a in range(3)]
+    grid = [[jnp.where(here.h == 1, row[b], row[2 - b]) for b in range(3)] for row in grid]
+    return lanes(*[grid[k // 3][k % 3] * kept[NEAR + k : NEAR + k + 1] for k in range(9)])
 
 
 def row_kernel(row, sides, chunk, boxes, out):
@@ -368,8 +358,8 @@
         out[4 + a] = row[2 + a]
 
 
-def first_kernel(got, boxes, base, couple, part):
-    part[...] = base[...] - dot(around(Here(), got, boxes), couple[...])
+def first_kernel(got, boxes, base, kept, couple, part):
+    part[...] = base[...] - dot(around(Here(), got, boxes, kept), couple[...])
 
 
 def put_together(here, kept, sides, row, whole):
@@ -509,9 +499,10 @@
     fill(here, boxes, chunk)
 
 
-def last_kernel(got, boxes, kept, adjoint, shares):
-    here = Here()
-    rest = kept[ZONE_ONE:] - dot(around(here, got, boxes), kept[LIFT_ONE : LIFT_ONE + 9 * SKEL])
+def last_kernel(got, boxes, kept, spread, adjoint, shares):
+    here = Here()
+    rest = kept[ZONE_ONE:NEAR] - dot(around(here, got, boxes, kept), spread[...])
+    rest = rest - dot(boxes[0], kept[BACK_ONE : BACK_ONE + SKEL])
     final = place(lanes(boxes[0], rest), numbers_of(kept, NUMBERS + ORDER_ONE))
     result = lanes(dot(final, kept[LEAF : LEAF + BOX]), dot(final, kept[LEAF + BOX : LEAF + 2 * BOX]))
     adjoint[...] = result
@@ -555,7 +546,7 @@
 def start(arrays):
     outs = [
         pltpu.VMEM(shape, jnp.float32)
-        for shape in (VALUES, VALUES, (5, *BLOCK), (3 * SKEL + 8, SKEL), (9 * SKEL, SKEL), KEPT)
+        for shape in (VALUES, VALUES, (5, *BLOCK), (3 * SKEL + 8, SKEL), KEPT)
     ]
     return pl.pallas_call(
         start_kernel,
@@ -587,7 +578,8 @@
     def from_row(blocks):
         return lax.ppermute(blocks, "by", [(i, i ^ 1) for i in range(lax.axis_size("by"))])
 
-    zone_one, base, to_row, to_side, couple, kept = start(arrays)
+    couple, spread = (arrays[name].reshape(9 * SKEL, SKEL) for name in ("couple_one", "spread_one"))
+    zone_one, base, to_row, to_side, kept = start(arrays)
     pair = lax.all_gather(zone_one, AXES, axis_index_groups=groups.diagonal)
     to_side = call(side_kernel, [SIDE], pair, to_side)
     sides = lax.all_gather(to_side, AXES, axis_index_groups=groups.sibling)
@@ -595,7 +587,7 @@
         row_kernel, [(4, 2, *VALUES), (4, *VALUES), (7, *BLOCK)], to_row, sides
     )
     row = from_row(to_row)
-    part = call(first_kernel, [VALUES], outside(chunk), boxes, base, couple)
+    part = call(first_kernel, [VALUES], outside(chunk), boxes, base, kept, couple)
 
     one, two, three = [(4, *VALUES), VALUES, VALUES], [(4, 2, *VALUES), VALUES, VALUES], [VALUES]
     chunk, base, zone_two, whole = call(second_kernel, two + [WHOLE], shared(part), kept, sides, row)
@@ -612,7 +604,7 @@
     part = call(up_two, three, outside(chunk), chunk, base, kept, whole)
     chunk, boxes = call(back_two_kernel, [(4, 2, *VALUES), (4, *VALUES)], shared(part), chunk, kept, whole)
     count = lax.axis_size("rhs")
-    adjoint, shares = call(last_kernel, [(COLS, BOX), (count, 8, SKEL)], outside(chunk), boxes, kept)
+    adjoint, shares = call(last_kernel, [(COLS, BOX), (count, 8, SKEL)], outside(chunk), boxes, kept, spread)
     shares = lax.all_to_all(shares, "rhs", 0, 0)
     adjoint, gradient = pl.pallas_call(
         end_kernel,

time: 108 us -> 108 us (level)
  no operation moved by 1% of the time
where the time goes in v4:
time: 108 us; the launch traced here: 107 us
  blocking collectives  98.2 us (91%)
  Pallas kernels  6.31 us (6%)
  starting transfers between devices  2.08 us (2%)
    all_to_all x6, blocking collectives, outside(): return lax.all_to_all(chunk, AXES, 0, 0, axis_index_groups=members)  54.8 us
    all_gather x5, blocking collectives, shared(): pair = lax.all_gather(part, AXES, axis_index_groups=groups.diagonal)  19 us
    all_to_all x1, blocking collectives, on_device(): shares = lax.all_to_all(shares, 'rhs', 0, 0)  9.35 us
    all_gather x5, blocking collectives, shared(): return lax.all_gather(pair, AXES, axis_index_groups=groups.sibling)  9.09 us
    all_gather x1, blocking collectives, on_device(): pair = lax.all_gather(zone_one, AXES, axis_index_groups=groups.diagonal)  3.86 us
    pallas_call x13, Pallas kernels, call(): pl.pallas_call(body, out_shape=outs, in_specs=spec(pltpu.VMEM, len(operan...  3.41 us
    pallas_call x1, Pallas kernels, start(): pl.pallas_call(start_kernel, out_shape=tuple(outs), in_specs=spec(pl.ANY,...  2.28 us
  transfers between devices with their start and end apart: 1, of which 0 were waited for; matrix products, arithmetic and copies ran while one was open for 0% of the time, Pallas kernels for 0%

profile of v4, /device:TPU:96, one launch (start us, length us, event | category | flops | bytes accessed | tf_op | source)
XLA Modules:
  0.0 107.3 jit_solution(1955722044841630233)
XLA Ops:
  0.6 2.3 %shard_map.248 = (f32[16,128]{1,0:T(8,128)S(1)}, f32[16,128]{1,0:T(8,128)S(1)}, f32[5,128,128]{2,1,0:T(8,128)S(1)}, f32[392,128]{1,0:T(8,128)S(1)}, f32[1896,128]{1,0:T(8,128)S(1)}) custom-call(f32[16,256]{1,0:T(8,128)} %bitcast.88, f32[256,256]{1,0:T(8,128)} %bitcast.73, s32[1,256]{1,0:T(1,128)} %bitcast.94, f32[128,128]{1,0:T(8,128)} %bitcast.77, ...), custom_call_target="tpu_custom_call" | custom-call | tf_op jit(solution)/shard_map/pallas_call | solution.py:551
  2.9 3.9 %all-gather = f32[32,128]{1,0:T(8,128)S(1)} all-gather(f32[16,128]{1,0:T(8,128)S(1)} %get-tuple-element.28), channel_id=2, replica_groups={{0,68},{1,69},{2,70},{3,71},{4,64},{5,65},{6,66},{7,67},{8,76},{9,77},{..., dimensions={0}, use_global_device_ids=true | all-gather | bytes 24576 | tf_op jit(solution)/shard_map/all_gather | solution.py:583
  6.8 2.1 %all-gather.1 = f32[848,128]{1,0:T(8,128)S(1)} all-gather(f32[424,128]{1,0:T(8,128)S(1)} %shard_map.249), channel_id=3, replica_groups={{0,64},{1,65},{2,66},{3,67},{4,68},{5,69},{6,70},{7,71},{8,72},{9,73},{..., dimensions={0}, use_global_device_ids=true | all-gather | bytes 651264 | tf_op jit(solution)/shard_map/all_gather | solution.py:585
  8.9 0.0 copy-start
  9.0 2.1 %collective-permute-start = (f32[7,128,128]{2,1,0:T(8,128)S(1)}, f32[7,128,128]{2,1,0:T(8,128)S(1)}, u32[]{:S(2)}, u32[]{:S(2)}) collective-permute-start(f32[7,128,128]{2,1,0:T(8,128)S(1)} %get-tuple-element.34), channel_id=1, source_target_pairs={{0,4},{4,0},{8,12},{12,8},{16,20},{20,16},{24,28},{28,24},{32,36},... | collective-permute-start | bytes 1376264 | tf_op jit(solution)/shard_map/ppermute | solution.py:579
  11.1 13.1 %all_to_all.35.got = f32[4,2,16,128]{3,2,1,0:T(8,128)S(1)} all-to-all(f32[4,2,16,128]{3,2,1,0:T(8,128)S(1)} %get-tuple-element.30), channel_id=1, replica_groups={{68,132,72,136},{196,260,200,264},{324,388,328,392},{4,5,8,9},{452,453,..., dimensions={0} | all-to-all | bytes 131072 | tf_op jit(solution)/shard_map/all_to_all | solution.py:572
  24.2 0.0 copy-done
  24.2 0.2 shard_map.251
  24.5 3.8 %all-gather.2 = f32[32,128]{1,0:T(8,128)S(1)} all-gather(f32[16,128]{1,0:T(8,128)S(1)} %shard_map.251), channel_id=4, replica_groups={{0,68},{1,69},{2,70},{3,71},{4,64},{5,65},{6,66},{7,67},{8,76},{9,77},{..., dimensions={0}, use_global_device_ids=true | all-gather | bytes 24576 | tf_op jit(solution)/shard_map/all_gather | solution.py:575
  28.3 1.8 %all-gather.3 = f32[4,16,128]{2,1,0:T(8,128)S(1)} all-gather(f32[2,16,128]{2,1,0:T(8,128)S(1)} %bitcast.80), channel_id=5, replica_groups={{0,64},{1,65},{2,66},{3,67},{4,68},{5,69},{6,70},{7,71},{8,72},{9,73},{..., dimensions={0}, use_global_device_ids=true | all-gather | bytes 49152 | tf_op jit(solution)/shard_map/all_gather | solution.py:576
  30.1 0.0 collective-permute-done.row
  30.1 0.4 shard_map.252
  30.5 8.4 %all_to_all.36.got = f32[4,2,16,128]{3,2,1,0:T(8,128)S(1)} all-to-all(f32[4,2,16,128]{3,2,1,0:T(8,128)S(1)} %get-tuple-element.35.chunk), channel_id=1, replica_groups={{68,132,72,136},{196,260,200,264},{324,388,328,392},{4,5,8,9},{452,453,..., dimensions={0} | all-to-all | bytes 131072 | tf_op jit(solution)/shard_map/all_to_all | solution.py:572
  39.0 0.3 shard_map.253
  39.3 3.8 %all-gather.4 = f32[32,128]{1,0:T(8,128)S(1)} all-gather(f32[16,128]{1,0:T(8,128)S(1)} %shard_map.253), channel_id=6, replica_groups={{0,68},{1,69},{2,70},{3,71},{4,64},{5,65},{6,66},{7,67},{8,76},{9,77},{..., dimensions={0}, use_global_device_ids=true | all-gather | bytes 24576 | tf_op jit(solution)/shard_map/all_gather | solution.py:575
  43.1 1.8 %all-gather.5 = f32[4,16,128]{2,1,0:T(8,128)S(1)} all-gather(f32[2,16,128]{2,1,0:T(8,128)S(1)} %bitcast.81), channel_id=7, replica_groups={{0,64},{1,65},{2,66},{3,67},{4,68},{5,69},{6,70},{7,71},{8,72},{9,73},{..., dimensions={0}, use_global_device_ids=true | all-gather | bytes 49152 | tf_op jit(solution)/shard_map/all_gather | solution.py:576
  44.9 0.4 shard_map.254
  45.3 8.5 %all_to_all.37.got = f32[4,16,128]{2,1,0:T(8,128)S(1)} all-to-all(f32[4,16,128]{2,1,0:T(8,128)S(1)} %get-tuple-element.38), channel_id=1, replica_groups={{68,132,8,200},{196,260,136,328},{324,388,264,456},{4,5,72,73},{452,453..., dimensions={0} | all-to-all | bytes 65536 | tf_op jit(solution)/shard_map/all_to_all | solution.py:572
  53.7 0.2 shard_map.255
  53.9 3.8 %all-gather.6 = f32[32,128]{1,0:T(8,128)S(1)} all-gather(f32[16,128]{1,0:T(8,128)S(1)} %shard_map.255), channel_id=8, replica_groups={{0,68},{1,69},{2,70},{3,71},{4,64},{5,65},{6,66},{7,67},{8,76},{9,77},{..., dimensions={0}, use_global_device_ids=true | all-gather | bytes 24576 | tf_op jit(solution)/shard_map/all_gather | solution.py:575
  57.7 1.8 %all-gather.7 = f32[4,16,128]{2,1,0:T(8,128)S(1)} all-gather(f32[2,16,128]{2,1,0:T(8,128)S(1)} %bitcast.82), channel_id=9, replica_groups={{0,64},{1,65},{2,66},{3,67},{4,68},{5,69},{6,70},{7,71},{8,72},{9,73},{..., dimensions={0}, use_global_device_ids=true | all-gather | bytes 49152 | tf_op jit(solution)/shard_map/all_gather | solution.py:576
  59.5 0.3 shard_map.256
  59.8 7.8 %all_to_all.38.got = f32[4,16,128]{2,1,0:T(8,128)S(1)} all-to-all(f32[4,16,128]{2,1,0:T(8,128)S(1)} %get-tuple-element.41.values), channel_id=1, replica_groups={{68,132,8,200},{196,260,136,328},{324,388,264,456},{4,5,72,73},{452,453..., dimensions={0} | all-to-all | bytes 65536 | tf_op jit(solution)/shard_map/all_to_all | solution.py:572
  67.6 0.2 shard_map.257
  67.8 3.8 %all-gather.8 = f32[32,128]{1,0:T(8,128)S(1)} all-gather(f32[16,128]{1,0:T(8,128)S(1)} %shard_map.257), channel_id=10, replica_groups={{0,68},{1,69},{2,70},{3,71},{4,64},{5,65},{6,66},{7,67},{8,76},{9,77},{..., dimensions={0}, use_global_device_ids=true | all-gather | bytes 24576 | tf_op jit(solution)/shard_map/all_gather | solution.py:575
  71.6 1.8 %all-gather.9 = f32[4,16,128]{2,1,0:T(8,128)S(1)} all-gather(f32[2,16,128]{2,1,0:T(8,128)S(1)} %bitcast.83), channel_id=11, replica_groups={{0,64},{1,65},{2,66},{3,67},{4,68},{5,69},{6,70},{7,71},{8,72},{9,73},{..., dimensions={0}, use_global_device_ids=true | all-gather | bytes 49152 | tf_op jit(solution)/shard_map/all_gather | solution.py:576
  73.4 0.2 shard_map.258
  73.6 8.5 %all_to_all.39.got = f32[4,2,16,128]{3,2,1,0:T(8,128)S(1)} all-to-all(f32[4,2,16,128]{3,2,1,0:T(8,128)S(1)} %get-tuple-element.44.chunk.values), channel_id=1, replica_groups={{68,132,72,136},{196,260,200,264},{324,388,328,392},{4,5,8,9},{452,453,..., dimensions={0} | all-to-all | bytes 131072 | tf_op jit(solution)/shard_map/all_to_all | solution.py:572
  82.1 0.3 shard_map.259
  82.4 3.8 %all-gather.10 = f32[32,128]{1,0:T(8,128)S(1)} all-gather(f32[16,128]{1,0:T(8,128)S(1)} %shard_map.259), channel_id=12, replica_groups={{0,68},{1,69},{2,70},{3,71},{4,64},{5,65},{6,66},{7,67},{8,76},{9,77},{..., dimensions={0}, use_global_device_ids=true | all-gather | bytes 24576 | tf_op jit(solution)/shard_map/all_gather | solution.py:575
  86.2 1.8 %all-gather.11 = f32[4,16,128]{2,1,0:T(8,128)S(1)} all-gather(f32[2,16,128]{2,1,0:T(8,128)S(1)} %bitcast.84), channel_id=13, replica_groups={{0,64},{1,65},{2,66},{3,67},{4,68},{5,69},{6,70},{7,71},{8,72},{9,73},{..., dimensions={0}, use_global_device_ids=true | all-gather | bytes 49152 | tf_op jit(solution)/shard_map/all_gather | solution.py:576
  88.0 0.0 copy-start.1
  88.0 0.2 shard_map.260
  88.2 8.4 %all_to_all.40.got = f32[4,2,16,128]{3,2,1,0:T(8,128)S(1)} all-to-all(f32[4,2,16,128]{3,2,1,0:T(8,128)S(1)} %get-tuple-element.46), channel_id=1, replica_groups={{68,132,72,136},{196,260,200,264},{324,388,328,392},{4,5,8,9},{452,453,..., dimensions={0} | all-to-all | bytes 131072 | tf_op jit(solution)/shard_map/all_to_all | solution.py:572
  96.7 0.0 copy-done.1
  96.7 0.7 shard_map.261
  97.3 9.4 %all_to_all.41.shares = f32[4,8,128]{2,1,0:T(8,128)S(1)} all-to-all(f32[4,8,128]{2,1,0:T(8,128)S(1)} %get-tuple-element.49), channel_id=1, replica_groups=mesh['bx'=8,'by'=16,'rhs'=4] {'rhs'}, dimensions={0} | all-to-all | bytes 32768 | tf_op jit(solution)/shard_map/all_to_all | solution.py:608
  106.7 0.6 shard_map.262
  (2 shorter events, 0.1 us)
Async XLA Ops:
  8.9 15.3 %copy-start = (f32[1,1,9,128,128]{4,3,2,1,0:T(8,128)S(1)}, f32[1,1,9,128,128]{4,3,2,1,0:T(8,128)}, u32[]{:S(2)}) copy-start(f32[1,1,9,128,128]{4,3,2,1,0:T(8,128)} %param.34) | copy-start | bytes 1769476
  9.0 21.1 %collective-permute-start = (f32[7,128,128]{2,1,0:T(8,128)S(1)}, f32[7,128,128]{2,1,0:T(8,128)S(1)}, u32[]{:S(2)}, u32[]{:S(2)}) collective-permute-start(f32[7,128,128]{2,1,0:T(8,128)S(1)} %get-tuple-element.34), channel_id=1, source_target_pairs={{0,4},{4,0},{8,12},{12,8},{16,20},{20,16},{24,28},{28,24},{32,36},... | collective-permute-start | bytes 1376264 | tf_op jit(solution)/shard_map/ppermute | solution.py:579
  88.0 8.6 %copy-start.1 = (f32[1,1,9,128,128]{4,3,2,1,0:T(8,128)S(1)}, f32[1,1,9,128,128]{4,3,2,1,0:T(8,128)}, u32[]{:S(2)}) copy-start(f32[1,1,9,128,128]{4,3,2,1,0:T(8,128)} %param.36) | copy-start | bytes 1769476
